TPU v7x, 512 devices: a whole 4x4x16 slice. The times are simulated.
512 devices in a mesh: section: 8 (over z_hi, x), feat: 64 (over y, z_lo, core).
Axes of the slice: x: 4, y: 4, z: 16 (z_hi: 2, z_lo: 8; z = z_hi * 8 + z_lo), core: 2. Of those that a mesh axis runs over, the one named last changes fastest.
Arguments:
- pre_tiles: bfloat16 [8, 256, 32, 128], P('section', 'feat'), may hold values from -6 to 6
- block_ids: int32 [8, 256, 32], P('section', 'feat'), may hold values from 0 to 127, all different within a row
- thresholds: float32 [8, 16384], P('section'), may hold values from 0.05 to 1
- decoder: bfloat16 [8, 16384, 2, 2048], P('section', 'feat'), may hold values from -0.09375 to 0.09375
- dec_bias: float32 [8, 2048], P('section'), may hold values from -3 to 3
- targets: bfloat16 [8, 256, 2048], P('section', 'feat'), may hold values from -6 to 6
Outputs:
- grad_tiles: bfloat16 [8, 256, 32, 128], P('section', 'feat')
- grad_decoder: bfloat16 [8, 16384, 2, 2048], P('section', 'feat')
Inputs may be any that keep to these rules, and one draw needn't show every extreme that they name: `block_ids`: the 32 block numbers of one token in one layer are distinct.
All inputs are finite; a program needn't handle non-finite values.
Results may differ from a plain program's by a relative error of at most 0.0042.
Values may be sent and summed in bfloat16 or wider, within the bound.
No kernel may reach another device: no remote copies, remote signals or barrier semaphores. Data moves between devices by JAX's collectives and lax.ppermute only.
A program may use at most 64 MiB of HBM per device.

v0:
```python
import jax
import jax.numpy as jnp
from jax import lax
from jax.sharding import PartitionSpec as P

BLK = 128


def from_behind(block, axis, distance):
    devices = range(lax.axis_size(axis))
    route = [(i - distance, i) for i in devices if i - distance in devices]
    return lax.ppermute(block, axis, route)


def per_device(pre_tiles, block_ids, thresholds, decoder, dec_bias, targets):
    feat_index = lax.axis_index("feat")
    feat_dev = decoder.shape[1]
    own_blocks = feat_dev // BLK
    tok_local = targets.shape[1]
    width = targets.shape[2]
    all_tiles, all_blocks = (
        lax.all_gather(pre_tiles[0], "feat", axis=0, tiled=True),
        lax.all_gather(block_ids[0], "feat", axis=0, tiled=True),
    )
    local_block = all_blocks - feat_index * own_blocks
    selector = (
        local_block[:, :, None] == jnp.arange(own_blocks, dtype=jnp.int32)[None, None, :]
    ).astype(jnp.bfloat16)
    dense = jnp.einsum("tkb,tkc->tbc", selector, all_tiles, preferred_element_type=jnp.float32)
    dense = dense.reshape(dense.shape[0], feat_dev)
    own_floor = lax.dynamic_slice_in_dim(thresholds[0], feat_index * feat_dev, feat_dev, 0)
    features = jnp.where(dense > own_floor[None, :], dense, 0.0).astype(jnp.bfloat16)
    weights = decoder[0].reshape(feat_dev, 2 * width)
    rows_part = features
    summed = lax.psum_scatter(
        jnp.dot(rows_part, weights, preferred_element_type=jnp.float32),
        "feat",
        scatter_dimension=0,
        tiled=True,
    )
    own_part = summed[:, :width]
    next_part = summed[:, width:]
    carried = from_behind(next_part, "section", 1)
    recon = own_part + carried + dec_bias[0][None, :]
    error_rows = (recon - targets[0].astype(jnp.float32)).astype(jnp.bfloat16)
    error_next = from_behind(error_rows, "section", -1)
    extended = jnp.concatenate([error_rows, error_next], axis=1)
    piece = lax.all_gather(extended, "feat", axis=0, tiled=True)
    rows_part = features
    dec_total = lax.dot_general(
        rows_part, piece, (((0,), (0,)), ((), ())), preferred_element_type=jnp.float32
    )
    block_grad = lax.dot_general(
        piece, weights, (((1,), (1,)), ((), ())), preferred_element_type=jnp.float32
    )
    feat_total = block_grad
    dec_total, feat_total = (dec_total, feat_total)
    grad_decoder = dec_total.astype(jnp.bfloat16).reshape(1, feat_dev, 2, width)
    feature_grad = feat_total.astype(jnp.bfloat16)
    token_grads = lax.all_to_all(feature_grad, "feat", split_axis=0, concat_axis=1, tiled=True)
    table = token_grads.reshape(tok_local, token_grads.shape[1] // BLK, BLK)
    block_list = block_ids[0]
    picked = jnp.take_along_axis(table, block_list[:, :, None], axis=1)
    floor_table = thresholds[0].reshape(thresholds.shape[1] // BLK, BLK)
    tile_floor = floor_table[block_list]
    gate_open = pre_tiles[0] > tile_floor
    grad_tiles = jnp.where(gate_open, picked, jnp.zeros_like(picked))
    return (grad_tiles[None], grad_decoder)


def solution(mesh):
    placed = (
        P("section", "feat", None, None),
        P("section", "feat", None),
        P("section", None),
        P("section", "feat", None, None),
        P("section", None),
        P("section", "feat", None),
    )
    return jax.shard_map(
        per_device,
        mesh=mesh,
        in_specs=placed,
        out_specs=(P("section", "feat", None, None), P("section", "feat", None, None)),
        check_vma=False,
    )
```

profile of v0, /device:TPU:6, one launch (start us, length us, event | category | flops | bytes accessed | tf_op | source)
XLA Modules:
  0.0 1160.0 jit_solution(4436772188853869188)
XLA Ops:
  7.2 0.0 copy-start
  7.2 0.0 all-gather.6.cloned.1.call-start
  7.2 0.7 all-gather.6.cloned.1.call-update
  7.9 0.0 all-reduce.3.cloned.1.call-start
  8.0 0.0 copy-start.2
  8.0 2.5 copy.13
  10.5 0.0 copy-done.2
  10.5 126.5 %all-gather = s32[1,256,32]{2,0,1:T(1,128)S(1)} all-gather(s32[1,4,32]{2,0,1:T(1,128)S(1)} %bitcast.62), channel_id=2, replica_groups=mesh['section'=8,'feat'=64] {'feat'}, dimensions={1}, use_global_device_ids=true | all-gather | bytes 33280 | tf_op jit(solution)/shard_map/all_gather | solution.py:23
  136.9 0.0 copy-done
  137.0 0.0 all-gather.6.cloned.1.call-done
  137.0 2.3 fusion.4
  139.3 2.7 fusion.7
  142.0 0.0 copy-start.3
  142.0 0.0 copy-start.4
  142.0 0.0 all-reduce.3.cloned.1.call-update
  142.0 0.0 all-gather.8.cloned.1.call-start
  142.0 1.3 dynamic-slice.1
  144.0 835.6 %all-reduce.3.cloned.1.call-done = f32[256,4096]{1,0:T(8,128)} async-done(((f32[256,4096]{1,0:T(8,128)}), f32[256,4096]{1,0:T(8,128)}) %all-reduce.3.cloned.1.call-update) | async-done | bytes 4194320
  979.6 0.9 dynamic-slice.4
  980.5 12.0 %collective-permute-start = (f32[4,2048]{1,0:T(4,128)S(1)}, f32[4,2048]{1,0:T(4,128)S(1)}, u32[]{:S(2)}, u32[]{:S(2)}) collective-permute-start(f32[4,2048]{1,0:T(4,128)S(1)} %dynamic-slice.4), channel_id=1, source_target_pairs={{0,64},{64,128},{128,192},{192,256},{256,320},{320,384},{384,448},... | collective-permute-start | bytes 98312 | tf_op jit(solution)/shard_map/ppermute | solution.py:12
  992.5 1.6 collective-permute-done
  994.1 0.0 copy-done.3
  994.1 0.0 copy-done.4
  994.1 0.9 fusion.16
  995.0 1.9 collective-permute-start.1
  996.9 14.8 %collective-permute-done.1 = bf16[4,2048]{1,0:T(4,128)(2,1)S(1)} collective-permute-done((bf16[4,2048]{1,0:T(4,128)(2,1)S(1)}, bf16[4,2048]{1,0:T(4,128)(2,1)S(1)}, u32[]{:S(2)}, u32[]{:S(2)}) %collective-permute-start.1) | collective-permute-done | bytes 16416 | tf_op jit(solution)/shard_map/ppermute | solution.py:12
  1011.7 0.6 maximum_bitcast_fusion
  1012.4 0.0 all-gather.8.cloned.1.call-update
  1012.4 0.1 reshape.95
  1012.5 0.1 reshape.89
  1012.6 0.6 gather_fusion
  1013.2 109.0 %all-gather.8.cloned.1.call-done = bf16[64,4,4096]{2,1,0:T(4,128)(2,1)} async-done(((bf16[1,4,4096]{2,1,0:T(4,128)(2,1)}), bf16[64,4,4096]{2,1,0:T(4,128)(2,1)}) %all-gather.8.cloned.1.call-update) | async-done | bytes 2097168 | tf_op jit(solution)/shard_map/all_gather | solution.py:48
  1122.3 3.9 reshape.109
  1126.2 2.3 convolution_convert_fusion.1
  1128.5 0.7 all_to_all.12
  1129.2 7.5 all-to-all-start
  1136.8 2.3 convolution_convert_fusion
  1139.1 0.0 copy-start.1
  1139.1 2.8 reshape.85
  1141.9 9.7 all-to-all-done
  1151.7 1.1 gather_fusion.1
  1152.8 0.0 copy-done.1
  1152.8 0.7 fusion.13
  (7 shorter events, 0.1 us)
Async XLA Ops:
  7.2 129.8 %copy-start = (f32[1,16384]{1,0:T(1,128)S(1)}, f32[1,16384]{1,0:T(1,128)}, u32[]{:S(2)}) copy-start(f32[1,16384]{1,0:T(1,128)} %param.8) | copy-start | bytes 196612
  7.2 129.8 %all-gather.6.cloned.1.call-start = ((), (), s32[]{:S(2)}) async-start(), calls=%async_computation.1 | async-start | bytes 2129920 | tf_op jit(solution)/shard_map/all_gather | solution.py:22
  7.9 971.7 %all-reduce.3.cloned.1.call-start = ((), (), s32[]{:S(2)}) async-start(), calls=%async_computation.3 | async-start | bytes 8388608
  8.0 2.5 copy-start.2
  142.0 852.1 %copy-start.3 = (bf16[1,4,2048]{2,1,0:T(4,128)(2,1)S(1)}, bf16[1,4,2048]{2,1,0:T(4,128)(2,1)}, u32[]{:S(2)}) copy-start(bf16[1,4,2048]{2,1,0:T(4,128)(2,1)} %param.11) | copy-start | bytes 49156
  142.0 852.1 %copy-start.4 = (f32[1,2048]{1,0:T(1,128)S(1)}, f32[1,2048]{1,0:T(1,128)}, u32[]{:S(2)}) copy-start(f32[1,2048]{1,0:T(1,128)} %param.10) | copy-start | bytes 24580
  142.0 980.3 %all-gather.8.cloned.1.call-start = ((), (), s32[]{:S(2)}) async-start(), calls=%async_computation.2 | async-start | bytes 2129920 | tf_op jit(solution)/shard_map/all_gather | solution.py:48
  980.5 13.6 %collective-permute-start = (f32[4,2048]{1,0:T(4,128)S(1)}, f32[4,2048]{1,0:T(4,128)S(1)}, u32[]{:S(2)}, u32[]{:S(2)}) collective-permute-start(f32[4,2048]{1,0:T(4,128)S(1)} %dynamic-slice.4), channel_id=1, source_target_pairs={{0,64},{64,128},{128,192},{192,256},{256,320},{320,384},{384,448},... | collective-permute-start | bytes 98312 | tf_op jit(solution)/shard_map/ppermute | solution.py:12
  995.0 16.8 %collective-permute-start.1 = (bf16[4,2048]{1,0:T(4,128)(2,1)S(1)}, bf16[4,2048]{1,0:T(4,128)(2,1)S(1)}, u32[]{:S(2)}, u32[]{:S(2)}) collective-permute-start(bf16[4,2048]{1,0:T(4,128)(2,1)S(1)} %fusion.16), channel_id=1, source_target_pairs={{64,0},{128,64},{192,128},{256,192},{320,256},{384,320},{448,384},... | collective-permute-start | bytes 49160 | tf_op jit(solution)/shard_map/ppermute | solution.py:12
  1129.2 22.4 %all-to-all-start = ((bf16[64,4,256]{2,1,0:T(4,128)(2,1)}), bf16[64,4,256]{2,1,0:T(4,128)(2,1)S(1)}, u32[]{:S(2)}, u32[]{:S(2)}) async-start(bf16[64,4,256]{2,1,0:T(4,128)(2,1)} %all_to_all.12), calls=%async_computation | async-start | bytes 262144 | tf_op jit(solution)/shard_map/all_to_all | solution.py:60
  1139.1 13.7 %copy-start.1 = (bf16[1,4,32,128]{3,2,1,0:T(8,128)(2,1)S(1)}, bf16[1,4,32,128]{3,2,1,0:T(8,128)(2,1)}, u32[]{:S(2)}) copy-start(bf16[1,4,32,128]{3,2,1,0:T(8,128)(2,1)} %param.6) | copy-start | bytes 98308
Sparse Core Ops, SparseCore 0:
  10.2 125.1 all-gather.5
  142.1 837.4 all-reduce.2
  1012.5 109.6 all-gather.7
where the time goes:
time: 1160 us
  waiting for transfers between devices  971 us (84%)
  blocking collectives  126 us (11%)
  starting transfers between devices  21.6 us (2%)
  between operations  14.5 us (1%)
  local copies, waits for them, and re-layouts  14.1 us (1%)
    unnamed x4, waiting for transfers between devices  836 us
    all_gather x1, blocking collectives, per_device(): lax.all_gather(block_ids[0], 'feat', axis=0, tiled=True)  126 us
    all_gather x1, waiting for transfers between devices, per_device(): piece = lax.all_gather(extended, 'feat', axis=0, tiled=True)  109 us
  transfers between devices with their start and end apart: 6, of which 5 were waited for; matrix products, arithmetic and copies ran while one was open for 1% of the time, Pallas kernels for 0%

commit v1 on v0

v1 whole, which is shorter than its diff:
```python
import jax
import jax.numpy as jnp
from jax import lax
from jax.sharding import Mesh, PartitionSpec as P

BLK = 128
AXES = ("zh", "x", "y", "z", "c")
SIZES = (2, 4, 4, 8, 2)
SECTION, FEAT, CHIP = ("zh", "x"), ("y", "z", "c"), ("y", "z")
WIRE = jnp.float32


def swap_cores(block):
    return lax.ppermute(block, "c", [(0, 1), (1, 0)])


def exchange(block, axis):
    return lax.all_to_all(block, axis, split_axis=0, concat_axis=0, tiled=True)


def gather_rows(block, axis):
    copies = jnp.broadcast_to(block[None], (lax.axis_size(axis),) + block.shape)
    got = exchange(copies, axis)
    return got.reshape((-1,) + block.shape[1:])


def section_swap(block):
    route = []
    layers = SIZES[0] * SIZES[1]
    for layer in range(layers - 1):
        route.append((2 * layer + 1, 2 * layer + 2))
        route.append((2 * layer + 2, 2 * layer + 1))
    return lax.ppermute(block, ("zh", "x", "c"), route)


def per_device(pre_tiles, block_ids, thresholds, decoder, dec_bias, targets):
    bf16, f32 = jnp.bfloat16, jnp.float32
    core = lax.axis_index("c")
    layer = lax.axis_index(SECTION)
    last_layer = SIZES[0] * SIZES[1] - 1
    chips = SIZES[2] * SIZES[3]
    tiles, ids = pre_tiles[0], block_ids[0]
    tok_local = tiles.shape[0]
    blocks = thresholds.shape[1] // BLK
    feat_dev = decoder.shape[1]
    width = decoder.shape[3]

    weights = decoder[0]
    w_mine = lax.dynamic_index_in_dim(weights, core, 1, keepdims=False)
    w_other = lax.dynamic_index_in_dim(weights, 1 - core, 1, keepdims=False)
    w_partner = swap_cores(w_other)
    partner_targets = swap_cores(targets[0])

    selector = (ids[:, :, None] == jnp.arange(blocks, dtype=jnp.int32)[None, None, :]).astype(bf16)
    dense = jnp.einsum("tkb,tkc->tbc", selector, tiles, preferred_element_type=f32)
    floor = thresholds[0].reshape(blocks, BLK)
    own_rows = jnp.where(dense > floor[None], dense, 0.0).astype(bf16)
    own_rows = own_rows.reshape(tok_local, chips, 2 * feat_dev).transpose(1, 0, 2)
    half = exchange(own_rows, CHIP)
    other_half = swap_cores(half)
    first = jnp.where(core == 0, half, other_half)
    second = jnp.where(core == 0, other_half, half)
    features = jnp.concatenate([first, second], axis=1).reshape(-1, 2 * feat_dev)
    tokens = features.shape[0]
    f_mine = lax.dynamic_slice_in_dim(features, core * feat_dev, feat_dev, 1)
    f_other = lax.dynamic_slice_in_dim(features, (1 - core) * feat_dev, feat_dev, 1)

    part = jnp.dot(f_mine, w_mine, preferred_element_type=f32)
    part = part + jnp.dot(f_other, w_partner, preferred_element_type=f32)
    part = part.astype(WIRE).reshape(SIZES[2], tokens // SIZES[2], width)
    part = jnp.sum(exchange(part, "y").astype(f32), axis=0)
    part = part.astype(WIRE).reshape(SIZES[3], -1, width)
    part = jnp.sum(exchange(part, "z").astype(f32), axis=0)

    rows = jnp.concatenate([targets[0], partner_targets], axis=0).astype(f32)
    shift = jnp.where(core == 0, dec_bias[0][None, :] - rows, 0.0)
    mine = part + shift
    error = mine + section_swap(mine)
    error = jnp.where((core == 1) & (layer == last_layer), 0.0, error).astype(bf16)

    e_mine = gather_rows(gather_rows(error, "z"), "y")
    e_other = swap_cores(e_mine)

    contract = (((1,), (1,)), ((), ()))
    grad = lax.dot_general(e_mine, w_mine, contract, preferred_element_type=f32)
    grad = grad + lax.dot_general(e_other, w_other, contract, preferred_element_type=f32)
    grad = jnp.where(f_mine > 0, grad, 0.0).astype(bf16)
    returned = exchange(grad.reshape(2 * chips, tok_local, feat_dev), FEAT)

    e_first = jnp.where(core == 0, e_mine, e_other)
    e_second = jnp.where(core == 0, e_other, e_mine)
    extended = jnp.concatenate([e_first, e_second], axis=1)
    dec = lax.dot_general(f_mine, extended, (((0,), (0,)), ((), ())), preferred_element_type=f32)
    grad_decoder = dec.astype(bf16).reshape(1, feat_dev, 2, width)

    table = returned.transpose(1, 0, 2).reshape(tok_local, blocks, BLK)
    picked = jnp.einsum("tkb,tbc->tkc", selector, table, preferred_element_type=f32)
    return picked.astype(bf16)[None], grad_decoder


def solution(mesh):
    split = Mesh(mesh.devices.reshape(SIZES), AXES)
    placed = (
        P(SECTION, FEAT, None, None),
        P(SECTION, FEAT, None),
        P(SECTION, None),
        P(SECTION, FEAT, None, None),
        P(SECTION, None),
        P(SECTION, FEAT, None),
    )
    return jax.shard_map(
        per_device,
        mesh=split,
        in_specs=placed,
        out_specs=(P(SECTION, FEAT, None, None), P(SECTION, FEAT, None, None)),
        check_vma=False,
    )
```

time: 1160 us -> 179 us (0.15)
  waiting for transfers between devices: 971 us -> 48.9 us
  blocking collectives: 126 us -> 60 us
  starting transfers between devices: 21.6 us -> 45 us
  between operations: 14.5 us -> 0.91 us
    unnamed x4 -> x0, waiting for transfers between devices: 836 us -> none
    all_gather x1 -> x0, blocking collectives: 126 us -> none  [per_device(): lax.all_gather(block_ids[0], 'feat', axis=0, tiled=True)]
    all_gather x2 -> x0, waiting for transfers between devices: 109 us -> none  [the longest x1 109 us: per_device(): piece = lax.all_gather(extended, 'feat', axis=0, tiled=True)]
    all_to_all x0 -> x3, blocking collectives: none -> 60 us  [exchange(): return lax.all_to_all(block, axis, split_axis=0, concat_axis=0, tiled=True)]
    all_to_all x1 -> x3, waiting for transfers between devices: 9.71 us -> 42.5 us  [exchange(): return lax.all_to_all(block, axis, split_axis=0, concat_axis=0, tiled=True)]
    all_to_all x1 -> x3, starting transfers between devices: 7.55 us -> 27.8 us  [exchange(): return lax.all_to_all(block, axis, split_axis=0, concat_axis=0, tiled=True)]
  transfers between devices with their start and end apart: 6 -> 8, of which waited for: 5 -> 6; matrix products, arithmetic and copies ran while one was open for 1% -> 7% of each run, Pallas kernels for 0% -> 0%
where the time goes in v1:
time: 179 us; the launch traced here: 177 us
  blocking collectives  60 us (34%)
  waiting for transfers between devices  48.9 us (27%)
  starting transfers between devices  45 us (25%)
  local copies, waits for them, and re-layouts  13.3 us (7%)
  matrix products  7.28 us (4%)
    all_to_all x3, blocking collectives, exchange(): return lax.all_to_all(block, axis, split_axis=0, concat_axis=0, tiled=True)  60 us
    all_to_all x3, waiting for transfers between devices, exchange(): return lax.all_to_all(block, axis, split_axis=0, concat_axis=0, tiled=True)  42.5 us
    all_to_all x3, starting transfers between devices, exchange(): return lax.all_to_all(block, axis, split_axis=0, concat_axis=0, tiled=True)  27.8 us
    ppermute x4, starting transfers between devices, swap_cores(): return lax.ppermute(block, 'c', [(0, 1), (1, 0)])  15.3 us
    dynamic_slice x1, local copies, waits for them, and re-layouts, per_device(): w_other = lax.dynamic_index_in_dim(weights, 1 - core, 1, keepdims=False)  6.54 us
    ppermute x1, waiting for transfers between devices, section_swap(): return lax.ppermute(block, ('zh', 'x', 'c'), route)  3.64 us
  transfers between devices with their start and end apart: 8, of which 6 were waited for; matrix products, arithmetic and copies ran while one was open for 7% of the time, Pallas kernels for 0%

profile of v1, /device:TPU:6, one launch (start us, length us, event | category | flops | bytes accessed | tf_op | source)
XLA Modules:
  0.0 176.8 jit_solution(9435016824818877304)
XLA Ops:
  0.6 0.0 copy-start
  0.6 0.7 copy-done
  1.4 1.2 fusion.6
  2.6 0.1 reshape.36
  2.7 0.8 copy.30
  3.4 15.5 %all-to-all-start = ((bf16[32,4,512]{2,1,0:T(4,128)(2,1)}), bf16[32,4,512]{2,1,0:T(4,128)(2,1)S(1)}, u32[]{:S(2)}, u32[]{:S(2)}) async-start(bf16[32,4,512]{2,1,0:T(4,128)(2,1)} %bitcast.32), calls=%async_computation | async-start | bytes 262144 | tf_op jit(solution)/shard_map/all_to_all | solution.py:18
  19.0 6.5 %constant_dynamic-slice_fusion = (bf16[1,256,1,2048]{3,2,1,0:T(2,128)(2,1)S(1)}, bf16[1,256,1,2048]{3,2,1,0:T(2,128)(2,1)S(1)}) fusion(bf16[1,256,2,2048]{3,2,1,0:T(2,128)(2,1)} %param.9, s32[]{:T(128)S(6)} %select_n.69, s32[]{:T(128)S(6)} %select_n.67), kind=kLoop, calls=%fused_computation.33 | loop fusion | bytes 4194312 | tf_op jit(solution)/shard_map/jit(dynamic_index_in_dim)/dynamic_slice | solution.py:50
  25.5 0.0 copy-start.1
  25.5 0.6 copy.29
  26.2 1.9 %collective-permute-start.1 = (bf16[256,2048]{1,0:T(8,128)(2,1)S(1)}, bf16[256,2048]{1,0:T(8,128)(2,1)}, u32[]{:S(2)}, u32[]{:S(2)}) collective-permute-start(bf16[256,2048]{1,0:T(8,128)(2,1)S(1)} %bitcast.38), channel_id=1, source_target_pairs={{0,1},{1,0},{2,3},{3,2},{4,5},{5,4},{6,7},{7,6},{8,9},{9,8},{10,11... | collective-permute-start | bytes 3145736 | tf_op jit(solution)/shard_map/ppermute | solution.py:14
  28.1 5.2 %all-to-all-done = bf16[32,4,512]{2,1,0:T(4,128)(2,1)S(1)} async-done(((bf16[32,4,512]{2,1,0:T(4,128)(2,1)}), bf16[32,4,512]{2,1,0:T(4,128)(2,1)S(1)}, u32[]{:S(2)}, u32[]{:S(2)}) %all-to-all-start) | async-done | bytes 131104 | tf_op jit(solution)/shard_map/all_to_all | solution.py:18
  33.3 1.9 %collective-permute-start = (bf16[32,4,512]{2,1,0:T(4,128)(2,1)S(1)}, bf16[32,4,512]{2,1,0:T(4,128)(2,1)S(1)}, u32[]{:S(2)}, u32[]{:S(2)}) collective-permute-start(bf16[32,4,512]{2,1,0:T(4,128)(2,1)S(1)} %all-to-all-done), channel_id=1, source_target_pairs={{0,1},{1,0},{2,3},{3,2},{4,5},{5,4},{6,7},{7,6},{8,9},{9,8},{10,11... | collective-permute-start | bytes 393224 | tf_op jit(solution)/shard_map/ppermute | solution.py:14
  35.2 1.3 collective-permute-done
  36.6 0.1 maximum_bitcast_fusion
  36.7 0.0 copy-done.1
  36.7 0.9 fusion.8
  37.6 0.0 collective-permute-done.1
  37.6 1.7 convolution_add_fusion
  39.3 29.4 %all_to_all.30 = f32[4,64,2048]{2,1,0:T(8,128)S(1)} all-to-all(f32[4,64,2048]{2,1,0:T(8,128)S(1)} %bitcast.37), channel_id=1, replica_groups=mesh['zh'=2,'x'=4,'y'=4,'z'=8,'c'=2] {'y'}, dimensions={0} | all-to-all | bytes 4194304 | tf_op jit(solution)/shard_map/all_to_all | solution.py:18
  68.7 0.0 copy-start.3
  68.7 0.0 copy-start.4
  68.7 0.9 reduce_sum.18
  69.6 6.1 %all-to-all-start.2 = ((f32[8,8,2048]{2,1,0:T(8,128)}), f32[8,8,2048]{2,1,0:T(8,128)S(1)}, u32[]{:S(2)}, u32[]{:S(2)}) async-start(f32[8,8,2048]{2,1,0:T(8,128)} %bitcast.42), calls=%async_computation.2 | async-start | bytes 1048576 | tf_op jit(solution)/shard_map/all_to_all | solution.py:18
  75.8 0.0 copy-done.3
  75.8 1.9 %collective-permute-start.2 = (bf16[4,2048]{1,0:T(4,128)(2,1)S(1)}, bf16[4,2048]{1,0:T(4,128)(2,1)S(1)}, u32[]{:S(2)}, u32[]{:S(2)}) collective-permute-start(bf16[4,2048]{1,0:T(4,128)(2,1)S(1)} %bitcast.49), channel_id=1, source_target_pairs={{0,1},{1,0},{2,3},{3,2},{4,5},{5,4},{6,7},{7,6},{8,9},{9,8},{10,11... | collective-permute-start | bytes 49160 | tf_op jit(solution)/shard_map/ppermute | solution.py:14
  77.7 26.2 %all-to-all-done.2 = f32[8,8,2048]{2,1,0:T(8,128)S(1)} async-done(((f32[8,8,2048]{2,1,0:T(8,128)}), f32[8,8,2048]{2,1,0:T(8,128)S(1)}, u32[]{:S(2)}, u32[]{:S(2)}) %all-to-all-start.2) | async-done | bytes 524320 | tf_op jit(solution)/shard_map/all_to_all | solution.py:18
  103.9 0.0 collective-permute-done.2
  103.9 0.0 copy-done.4
  104.0 1.9 %collective-permute-start.3 = (f32[8,2048]{1,0:T(8,128)S(1)}, f32[8,2048]{1,0:T(8,128)S(1)}, u32[]{:S(2)}, u32[]{:S(2)}) collective-permute-start(f32[8,2048]{1,0:T(8,128)S(1)} %select_add_fusion), channel_id=1, source_target_pairs={{1,64},{64,1},{65,128},{128,65},{129,192},{192,129},{193,256},{256... | collective-permute-start | bytes 196616 | tf_op jit(solution)/shard_map/ppermute | solution.py:33
  105.9 3.6 %collective-permute-done.3 = f32[8,2048]{1,0:T(8,128)S(1)} collective-permute-done((f32[8,2048]{1,0:T(8,128)S(1)}, f32[8,2048]{1,0:T(8,128)S(1)}, u32[]{:S(2)}, u32[]{:S(2)}) %collective-permute-start.3) | collective-permute-done | bytes 65568 | tf_op jit(solution)/shard_map/ppermute | solution.py:33
  109.6 0.0 copy-start.2
  109.6 17.4 %all_to_all.31 = bf16[8,8,2048]{2,1,0:T(8,128)(2,1)S(1)} all-to-all(bf16[8,8,2048]{2,1,0:T(8,128)(2,1)S(1)} %broadcast_in_dim.33), channel_id=1, replica_groups=mesh['zh'=2,'x'=4,'y'=4,'z'=8,'c'=2] {'z'}, dimensions={0} | all-to-all | bytes 524288 | tf_op jit(solution)/shard_map/all_to_all | solution.py:18
  127.0 0.1 broadcast_in_dim.35
  127.1 13.3 %all_to_all.32 = bf16[4,64,2048]{2,1,0:T(8,128)(2,1)S(1)} all-to-all(bf16[4,64,2048]{2,1,0:T(8,128)(2,1)S(1)} %broadcast_in_dim.35), channel_id=1, replica_groups=mesh['zh'=2,'x'=4,'y'=4,'z'=8,'c'=2] {'y'}, dimensions={0} | all-to-all | bytes 2097152 | tf_op jit(solution)/shard_map/all_to_all | solution.py:18
  140.4 9.5 %collective-permute-start.4 = (bf16[256,2048]{1,0:T(8,128)(2,1)S(1)}, bf16[256,2048]{1,0:T(8,128)(2,1)S(1)}, u32[]{:S(2)}, u32[]{:S(2)}) collective-permute-start(bf16[256,2048]{1,0:T(8,128)(2,1)S(1)} %bitcast.40), channel_id=1, source_target_pairs={{0,1},{1,0},{2,3},{3,2},{4,5},{5,4},{6,7},{7,6},{8,9},{9,8},{10,11... | collective-permute-start | bytes 3145736 | tf_op jit(solution)/shard_map/ppermute | solution.py:14
  149.9 0.0 copy-done.2
  150.0 0.8 fusion.7
  150.8 1.4 collective-permute-done.4
  152.2 1.1 fusion.4
  153.3 1.6 reshape.41
  154.9 6.1 %all-to-all-start.5 = ((bf16[64,4,256]{2,1,0:T(4,128)(2,1)}), bf16[64,4,256]{2,1,0:T(4,128)(2,1)S(1)}, u32[]{:S(2)}, u32[]{:S(2)}) async-start(bf16[64,4,256]{2,1,0:T(4,128)(2,1)} %reshape.41), calls=%async_computation.5 | async-start | bytes 262144 | tf_op jit(solution)/shard_map/all_to_all | solution.py:18
  161.0 0.2 broadcast_select_fusion.1
  161.3 0.7 convolution_convert_fusion
  162.0 0.0 copy-start.5
  162.0 2.8 %reshape.43 = bf16[1,256,2,2048]{3,2,1,0:T(2,128)(2,1)} reshape(bf16[256,4096]{1,0:T(8,128)(2,1)S(1)} %convolution_convert_fusion) | data formatting | bytes 4194304 | tf_op jit(solution)/shard_map/reshape | solution.py:94
  164.8 11.1 %all-to-all-done.5 = bf16[64,4,256]{2,1,0:T(4,128)(2,1)S(1)} async-done(((bf16[64,4,256]{2,1,0:T(4,128)(2,1)}), bf16[64,4,256]{2,1,0:T(4,128)(2,1)S(1)}, u32[]{:S(2)}, u32[]{:S(2)}) %all-to-all-start.5) | async-done | bytes 131104 | tf_op jit(solution)/shard_map/all_to_all | solution.py:18
  175.9 0.0 copy-done.5
  176.0 0.8 fusion.5
  (7 shorter events, 0.2 us)
Async XLA Ops:
  0.6 0.8 copy-start
  3.4 29.9 %all-to-all-start = ((bf16[32,4,512]{2,1,0:T(4,128)(2,1)}), bf16[32,4,512]{2,1,0:T(4,128)(2,1)S(1)}, u32[]{:S(2)}, u32[]{:S(2)}) async-start(bf16[32,4,512]{2,1,0:T(4,128)(2,1)} %bitcast.32), calls=%async_computation | async-start | bytes 262144 | tf_op jit(solution)/shard_map/all_to_all | solution.py:18
  25.5 11.2 %copy-start.1 = (bf16[1,256,1,2048]{3,2,1,0:T(2,128)(2,1)}, bf16[1,256,1,2048]{3,2,1,0:T(2,128)(2,1)S(1)}, u32[]{:S(2)}) copy-start(bf16[1,256,1,2048]{3,2,1,0:T(2,128)(2,1)S(1)} %get-tuple-element.5) | copy-start | bytes 3145732
  26.2 11.4 %collective-permute-start.1 = (bf16[256,2048]{1,0:T(8,128)(2,1)S(1)}, bf16[256,2048]{1,0:T(8,128)(2,1)}, u32[]{:S(2)}, u32[]{:S(2)}) collective-permute-start(bf16[256,2048]{1,0:T(8,128)(2,1)S(1)} %bitcast.38), channel_id=1, source_target_pairs={{0,1},{1,0},{2,3},{3,2},{4,5},{5,4},{6,7},{7,6},{8,9},{9,8},{10,11... | collective-permute-start | bytes 3145736 | tf_op jit(solution)/shard_map/ppermute | solution.py:14
  33.3 3.2 %collective-permute-start = (bf16[32,4,512]{2,1,0:T(4,128)(2,1)S(1)}, bf16[32,4,512]{2,1,0:T(4,128)(2,1)S(1)}, u32[]{:S(2)}, u32[]{:S(2)}) collective-permute-start(bf16[32,4,512]{2,1,0:T(4,128)(2,1)S(1)} %all-to-all-done), channel_id=1, source_target_pairs={{0,1},{1,0},{2,3},{3,2},{4,5},{5,4},{6,7},{7,6},{8,9},{9,8},{10,11... | collective-permute-start | bytes 393224 | tf_op jit(solution)/shard_map/ppermute | solution.py:14
  68.7 7.1 %copy-start.3 = (bf16[1,4,2048]{2,1,0:T(4,128)(2,1)S(1)}, bf16[1,4,2048]{2,1,0:T(4,128)(2,1)}, u32[]{:S(2)}) copy-start(bf16[1,4,2048]{2,1,0:T(4,128)(2,1)} %param.11) | copy-start | bytes 49156
  68.7 35.2 %copy-start.4 = (f32[1,2048]{1,0:T(1,128)S(1)}, f32[1,2048]{1,0:T(1,128)}, u32[]{:S(2)}) copy-start(f32[1,2048]{1,0:T(1,128)} %param.10) | copy-start | bytes 24580
  69.6 34.2 %all-to-all-start.2 = ((f32[8,8,2048]{2,1,0:T(8,128)}), f32[8,8,2048]{2,1,0:T(8,128)S(1)}, u32[]{:S(2)}, u32[]{:S(2)}) async-start(f32[8,8,2048]{2,1,0:T(8,128)} %bitcast.42), calls=%async_computation.2 | async-start | bytes 1048576 | tf_op jit(solution)/shard_map/all_to_all | solution.py:18
  75.8 28.1 %collective-permute-start.2 = (bf16[4,2048]{1,0:T(4,128)(2,1)S(1)}, bf16[4,2048]{1,0:T(4,128)(2,1)S(1)}, u32[]{:S(2)}, u32[]{:S(2)}) collective-permute-start(bf16[4,2048]{1,0:T(4,128)(2,1)S(1)} %bitcast.49), channel_id=1, source_target_pairs={{0,1},{1,0},{2,3},{3,2},{4,5},{5,4},{6,7},{7,6},{8,9},{9,8},{10,11... | collective-permute-start | bytes 49160 | tf_op jit(solution)/shard_map/ppermute | solution.py:14
  104.0 5.6 %collective-permute-start.3 = (f32[8,2048]{1,0:T(8,128)S(1)}, f32[8,2048]{1,0:T(8,128)S(1)}, u32[]{:S(2)}, u32[]{:S(2)}) collective-permute-start(f32[8,2048]{1,0:T(8,128)S(1)} %select_add_fusion), channel_id=1, source_target_pairs={{1,64},{64,1},{65,128},{128,65},{129,192},{192,129},{193,256},{256... | collective-permute-start | bytes 196616 | tf_op jit(solution)/shard_map/ppermute | solution.py:33
  109.6 40.4 %copy-start.2 = (bf16[1,256,1,2048]{3,2,1,0:T(2,128)(2,1)S(1)}, bf16[1,256,1,2048]{3,2,1,0:T(2,128)(2,1)}, u32[]{:S(2)}) copy-start(bf16[1,256,1,2048]{3,2,1,0:T(2,128)(2,1)} %copy-done.1) | copy-start | bytes 3145732
  140.4 11.8 %collective-permute-start.4 = (bf16[256,2048]{1,0:T(8,128)(2,1)S(1)}, bf16[256,2048]{1,0:T(8,128)(2,1)S(1)}, u32[]{:S(2)}, u32[]{:S(2)}) collective-permute-start(bf16[256,2048]{1,0:T(8,128)(2,1)S(1)} %bitcast.40), channel_id=1, source_target_pairs={{0,1},{1,0},{2,3},{3,2},{4,5},{5,4},{6,7},{7,6},{8,9},{9,8},{10,11... | collective-permute-start | bytes 3145736 | tf_op jit(solution)/shard_map/ppermute | solution.py:14
  154.9 20.9 %all-to-all-start.5 = ((bf16[64,4,256]{2,1,0:T(4,128)(2,1)}), bf16[64,4,256]{2,1,0:T(4,128)(2,1)S(1)}, u32[]{:S(2)}, u32[]{:S(2)}) async-start(bf16[64,4,256]{2,1,0:T(4,128)(2,1)} %reshape.41), calls=%async_computation.5 | async-start | bytes 262144 | tf_op jit(solution)/shard_map/all_to_all | solution.py:18
  162.0 13.9 %copy-start.5 = (s32[1,4,32]{2,1,0:T(4,128)S(1)}, s32[1,4,32]{2,1,0:T(4,128)}, u32[]{:S(2)}) copy-start(s32[1,4,32]{2,1,0:T(4,128)} %param.7) | copy-start | bytes 1540

commit v2 on v1

v2 whole, which is shorter than its diff:
```python
import functools

import jax
import jax.numpy as jnp
from jax import lax
from jax.experimental import pallas as pl
from jax.experimental.pallas import tpu as pltpu
from jax.sharding import Mesh, PartitionSpec as P

BLK = 128
AXES = ("zh", "x", "y", "z", "c")
SIZES = (2, 4, 4, 8, 2)
SECTION, FEAT = ("zh", "x"), ("y", "z", "c")
WIRE_Y = jnp.float32
WIRE_Z = jnp.float32


def swap_cores(block):
    return lax.ppermute(block, "c", [(0, 1), (1, 0)])


def exchange(block, axis):
    return lax.all_to_all(block, axis, split_axis=0, concat_axis=0, tiled=True)


def gather(block, axis):
    copies = jnp.broadcast_to(block[None], (lax.axis_size(axis),) + block.shape)
    return exchange(copies, axis)


def to_layer(block, distance):
    layers = SIZES[0] * SIZES[1]
    route = [(i, i + distance) for i in range(layers) if 0 <= i + distance < layers]
    return lax.ppermute(block, SECTION, route)


def column_blocks(error_ref, col):
    for z in range(error_ref.shape[1]):
        for r in range(error_ref.shape[3] // col):
            block = error_ref[:, z, :, r * col : (r + 1) * col]
            yield z, r, block.reshape(-1, col)


def grad_kernel(col, error_ref, *refs):
    *weight_refs, grad_ref, total = refs
    step = pl.program_id(0)
    feat_dev = weight_refs[0].shape[0]

    @pl.when(step == 0)
    def _():
        total[...] = jnp.zeros_like(total)

    for z, r, block in column_blocks(error_ref, col):
        for half in range(2):
            weight = weight_refs[2 * half + r][:, z * col : (z + 1) * col]
            total[:, half * feat_dev : (half + 1) * feat_dev] += lax.dot_general(
                block, weight, (((1,), (1,)), ((), ())), preferred_element_type=jnp.float32
            )

    @pl.when(step == pl.num_programs(0) - 1)
    def _():
        grad_ref[...] = total[...].astype(grad_ref.dtype)


def feature_grads(error, weights, weights_other):
    ny, nz, rows, both = error.shape
    feat_dev = weights.shape[0]
    steps = 4
    wide = weights.shape[1] // 2 // steps
    blocks = [
        pl.BlockSpec((feat_dev, wide), lambda j, r=r: (0, r * steps + j)) for r in range(2)
    ]
    return pl.pallas_call(
        functools.partial(grad_kernel, both // 2),
        grid=(steps,),
        in_specs=[pl.BlockSpec((ny, nz // steps, rows, both), lambda j: (0, j, 0, 0))] + 2 * blocks,
        out_specs=pl.BlockSpec((ny * rows, 2 * feat_dev), lambda j: (0, 0)),
        out_shape=jax.ShapeDtypeStruct((ny * rows, 2 * feat_dev), error.dtype),
        scratch_shapes=[pltpu.VMEM((ny * rows, 2 * feat_dev), jnp.float32)],
        compiler_params=pltpu.CompilerParams(vmem_limit_bytes=24 << 20),
        cost_estimate=pl.CostEstimate(
            flops=2 * error.size * 2 * feat_dev, bytes_accessed=5 << 20, transcendentals=0
        ),
    )(error, weights, weights, weights_other, weights_other)


def decoder_kernel(col, feature_ref, error_ref, other_ref, out_ref):
    half = feature_ref.shape[1] // 2
    for (z, r, block), (_, _, other) in zip(
        column_blocks(error_ref, col), column_blocks(other_ref, col)
    ):
        total = jnp.dot(feature_ref[:, :half], block, preferred_element_type=jnp.float32)
        total += jnp.dot(feature_ref[:, half:], other, preferred_element_type=jnp.float32)
        out_ref[r, :, z * col : (z + 1) * col] = total.astype(out_ref.dtype)


def decoder_grads(features, error, error_other):
    ny, nz, rows, both = error.shape
    feat_dev = features.shape[0]
    steps = 4
    block = pl.BlockSpec((ny, nz // steps, rows, both), lambda j: (0, j, 0, 0))
    width = nz * both // 2
    return pl.pallas_call(
        functools.partial(decoder_kernel, both // 2),
        grid=(steps,),
        in_specs=[pl.BlockSpec(features.shape, lambda j: (0, 0)), block, block],
        out_specs=pl.BlockSpec((2, feat_dev, width // steps), lambda j: (0, 0, j)),
        out_shape=jax.ShapeDtypeStruct((2, feat_dev, width), error.dtype),
        compiler_params=pltpu.CompilerParams(vmem_limit_bytes=24 << 20),
        cost_estimate=pl.CostEstimate(
            flops=4 * error.size * feat_dev, bytes_accessed=4 << 20, transcendentals=0
        ),
    )(features, error, error_other)


def per_device(pre_tiles, block_ids, thresholds, decoder, dec_bias, targets):
    bf16, f32 = jnp.bfloat16, jnp.float32
    ny, nz, nc = SIZES[2:]
    core = lax.axis_index("c")
    chip = lax.axis_index(("y", "z"))
    layer = lax.axis_index(SECTION)
    last_layer = SIZES[0] * SIZES[1] - 1
    tiles, ids = pre_tiles[0], block_ids[0]
    tok = tiles.shape[0]
    blocks = thresholds.shape[1] // BLK
    feat_dev = decoder.shape[1]
    width = decoder.shape[3]
    own_blocks = feat_dev // BLK
    col = width // nz

    order = jnp.arange(blocks, dtype=jnp.int32) ^ (core * own_blocks)
    selector = (ids[:, :, None] == order[None, None, :]).astype(bf16)
    dense = jnp.einsum("tkb,tkc->tbc", selector, tiles, preferred_element_type=f32)
    floor = thresholds[0].reshape(-1, nc, own_blocks, BLK)
    floor = jnp.where(core == 0, floor, floor[:, ::-1]).reshape(blocks, BLK)
    own = jnp.where(dense > floor[None], dense, 0.0).astype(bf16)
    sent = own.reshape(tok, ny * nz, nc * feat_dev).transpose(1, 0, 2)
    features = exchange(sent, ("y", "z")).reshape(ny * nz * tok, nc * feat_dev)
    f_mine, f_other = features[:, :feat_dev], features[:, feat_dev:]

    weights = lax.optimization_barrier(decoder[0].reshape(feat_dev, nc * width))
    weights_other = swap_cores(weights)

    part = jnp.dot(f_mine, weights, preferred_element_type=f32)
    part = part + jnp.dot(f_other, weights_other, preferred_element_type=f32)
    shift = dec_bias[0][None, :] - targets[0].astype(f32)
    shift = jnp.concatenate([shift, jnp.zeros_like(shift)], axis=1)
    here = jnp.arange(ny * nz)[:, None, None] == chip
    part = part + jnp.where(here, shift[None], 0.0).reshape(part.shape)
    part = part.astype(WIRE_Y).reshape(ny, nz * tok, nc * width)
    part = jnp.sum(exchange(part, "y").astype(f32), axis=0)
    part = part.reshape(nz * tok, nc, nz, col).transpose(2, 0, 1, 3).astype(WIRE_Z)
    part = jnp.sum(exchange(part.reshape(nz, nz * tok, nc * col), "z").astype(f32), axis=0)

    mine, beyond = part[:, :col], part[:, col:]
    got, got_next = lax.optimization_barrier((to_layer(beyond, 1), to_layer(mine, -1)))
    error_next = jnp.where(layer == last_layer, 0.0, beyond + got_next)
    error = jnp.concatenate([mine + got, error_next], axis=1).astype(bf16)

    error = gather(gather(error, "z"), "y").reshape(ny, nz, nz * tok, nc * col)
    error_other = swap_cores(error)

    grad = feature_grads(error, weights, weights_other).reshape(ny * nz, tok, -1)
    grad, error_other = lax.optimization_barrier((grad, error_other))
    returned = exchange(grad, ("y", "z"))

    f_own = jnp.concatenate([f_mine, swap_cores(f_other)], axis=0).T
    grad_decoder = decoder_grads(f_own, error, error_other).transpose(1, 0, 2)[None]

    table = returned.transpose(1, 0, 2).reshape(tok, blocks, BLK)
    table = jnp.where(own > 0, table, jnp.zeros_like(table))
    picked = jnp.einsum("tkb,tbc->tkc", selector, table, preferred_element_type=f32)
    return picked.astype(bf16)[None], grad_decoder


def solution(mesh):
    split = Mesh(mesh.devices.reshape(SIZES), AXES)
    placed = (
        P(SECTION, FEAT, None, None),
        P(SECTION, FEAT, None),
        P(SECTION, None),
        P(SECTION, FEAT, None, None),
        P(SECTION, None),
        P(SECTION, FEAT, None),
    )
    return jax.shard_map(
        per_device,
        mesh=split,
        in_specs=placed,
        out_specs=(P(SECTION, FEAT, None, None), P(SECTION, FEAT, None, None)),
        check_vma=False,
    )
```

time: 179 us -> 188 us (1.050)
  blocking collectives: 60 us -> 93.3 us
  waiting for transfers between devices: 48.9 us -> 17.2 us
  Pallas kernels: 0 us -> 7.21 us
  matrix products: 7.28 us -> 3.81 us
  starting transfers between devices: 45 us -> 48.1 us
    all_to_all x3 -> x4, blocking collectives: 60 us -> 93.3 us  [exchange(): return lax.all_to_all(block, axis, split_axis=0, concat_axis=0, tiled=True)]
    all_to_all x3 -> x2, waiting for transfers between devices: 42.5 us -> 14.7 us  [exchange(): return lax.all_to_all(block, axis, split_axis=0, concat_axis=0, tiled=True)]
    ppermute x1 -> x2, starting transfers between devices: 1.92 us -> 16.7 us  [to_layer(): return lax.ppermute(block, SECTION, route)]
    ppermute x4 -> x3, starting transfers between devices: 15.3 us -> 5.96 us  [swap_cores(): return lax.ppermute(block, 'c', [(0, 1), (1, 0)])]
    pallas_call x0 -> x2, Pallas kernels: none -> 7.21 us  [the longest x1 3.84 us: feature_grads(): pl.pallas_call(functools.partial(grad_kernel, both // 2), grid=(steps,),...]
    dynamic_slice x1 -> x0, local copies, waits for them, and re-layouts: 6.54 us -> none  [per_device(): w_other = lax.dynamic_index_in_dim(weights, 1 - core, 1, keepdims=False)]
    unnamed x13 -> x18, local copies, waits for them, and re-layouts: 1.39 us -> 7.55 us
    broadcast_in_dim x2 -> x6, local copies, waits for them, and re-layouts: 0.13 us -> 5.05 us  [the longest x4 4.92 us: per_device(): part = part + jnp.where(here, shift[None], 0.0).reshape(part.shape)]
  transfers between devices with their start and end apart: 8 -> 7, of which waited for: 6 -> 4; matrix products, arithmetic and copies ran while one was open for 7% -> 6% of each run, Pallas kernels for 0% -> 4%
where the time goes in v2:
time: 188 us
  blocking collectives  93.3 us (50%)
  starting transfers between devices  48.1 us (26%)
  waiting for transfers between devices  17.2 us (9%)
  local copies, waits for them, and re-layouts  15 us (8%)
  Pallas kernels  7.21 us (4%)
  matrix products  3.81 us (2%)
  other arithmetic  1.96 us (1%)
    all_to_all x4, blocking collectives, exchange(): return lax.all_to_all(block, axis, split_axis=0, concat_axis=0, tiled=True)  93.3 us
    all_to_all x2, starting transfers between devices, exchange(): return lax.all_to_all(block, axis, split_axis=0, concat_axis=0, tiled=True)  25.4 us
    ppermute x2, starting transfers between devices, to_layer(): return lax.ppermute(block, SECTION, route)  16.7 us
    all_to_all x2, waiting for transfers between devices, exchange(): return lax.all_to_all(block, axis, split_axis=0, concat_axis=0, tiled=True)  14.7 us
    unnamed x18, local copies, waits for them, and re-layouts  7.55 us
    ppermute x3, starting transfers between devices, swap_cores(): return lax.ppermute(block, 'c', [(0, 1), (1, 0)])  5.96 us
    broadcast_in_dim x4, local copies, waits for them, and re-layouts, per_device(): part = part + jnp.where(here, shift[None], 0.0).reshape(part.shape)  4.92 us
    pallas_call x1, Pallas kernels, feature_grads(): pl.pallas_call(functools.partial(grad_kernel, both // 2), grid=(steps,),...  3.84 us
  transfers between devices with their start and end apart: 7, of which 4 were waited for; matrix products, arithmetic and copies ran while one was open for 6% of the time, Pallas kernels for 4%

profile of v2, /device:TPU:6, one launch (start us, length us, event | category | flops | bytes accessed | tf_op | source)
XLA Modules:
  0.0 187.5 jit_solution(17839197234588944681)
XLA Ops:
  0.6 0.0 copy-start
  0.6 0.0 copy-start.2
  0.7 0.0 copy-start.5
  0.7 0.0 copy-start.3
  0.7 0.0 copy-start.4
  0.7 2.5 %copy.24 = bf16[32,8,2,2048]{3,1,2,0:T(8,128)(2,1)S(1)} copy(bf16[32,8,2,2048]{3,2,1,0:T(2,128)(2,1)} %bitcast.40) | data formatting | bytes 4194304
  3.2 1.9 %collective-permute-start = (bf16[256,4096]{1,0:T(8,128)(2,1)S(1)}, bf16[256,4096]{1,0:T(8,128)(2,1)}, u32[]{:S(2)}, u32[]{:S(2)}) collective-permute-start(bf16[256,4096]{1,0:T(8,128)(2,1)S(1)} %bitcast.34), channel_id=1, source_target_pairs={{0,1},{1,0},{2,3},{3,2},{4,5},{5,4},{6,7},{7,6},{8,9},{9,8},{10,11... | collective-permute-start | bytes 6291464 | tf_op jit(solution)/shard_map/ppermute | solution.py:19
  5.2 0.0 copy-done.2
  5.2 0.0 copy-done
  5.2 0.0 copy-done.5
  5.2 0.3 fusion.10
  5.6 0.1 fusion.11
  5.7 0.1 reshape.58
  5.8 0.8 copy.27
  6.5 15.5 %all-to-all-start = ((bf16[32,4,512]{2,1,0:T(4,128)(2,1)}), bf16[32,4,512]{2,1,0:T(4,128)(2,1)S(1)}, u32[]{:S(2)}, u32[]{:S(2)}) async-start(bf16[32,4,512]{2,1,0:T(4,128)(2,1)} %bitcast.33), calls=%async_computation | async-start | bytes 262144 | tf_op jit(solution)/shard_map/all_to_all | solution.py:23
  22.1 0.1 broadcast_in_dim.57
  22.2 0.1 broadcast_in_dim.58
  22.3 0.0 copy-done.3
  22.3 0.0 copy-done.4
  22.3 1.8 broadcast_in_dim.60
  24.1 2.9 %broadcast_in_dim.61 = f32[128,4096]{1,0:T(8,128)} reshape(f32[32,4,4096]{2,1,0:T(4,128)} %broadcast_in_dim.60) | data formatting | bytes 4194304 | tf_op jit(solution)/shard_map/jit(_where)/broadcast_in_dim | solution.py:149
  27.1 9.9 %all-to-all-done = bf16[32,4,512]{2,1,0:T(4,128)(2,1)S(1)} async-done(((bf16[32,4,512]{2,1,0:T(4,128)(2,1)}), bf16[32,4,512]{2,1,0:T(4,128)(2,1)S(1)}, u32[]{:S(2)}, u32[]{:S(2)}) %all-to-all-start) | async-done | bytes 131104 | tf_op jit(solution)/shard_map/all_to_all | solution.py:23
  37.0 0.0 copy-start.1
  37.0 0.4 fusion.22
  37.5 0.0 collective-permute-done.refs_2_.refs_3_
  37.5 1.1 copy-done.1
  38.6 2.2 %fusion = f32[128,4096]{1,0:T(8,128)S(1)} fusion(f32[128,4096]{1,0:T(8,128)S(1)} %fusion.22, bf16[256,4096]{1,0:T(8,128)(2,1)} %collective-permute-done.refs_2_.refs_3_, f32[128,4096]{1,0:T(8,128)S(1)} %copy-done.1, pred[128]{0:T(512)(128)(4,1)S(1)} %broadcast_in_dim.58, bf16[128,512]{1,0:T(8,128)(2,1)S(1)} %reshape.59), kind=kOutput, calls=%fused_computation.1 | convolution fusion | flops 270008320 | bytes 8454656 | tf_op jit(solution)/shard_map/dot_general | solution.py:145
  40.9 27.3 %all_to_all.30 = f32[4,32,4096]{2,1,0:T(8,128)} all-to-all(f32[4,32,4096]{2,1,0:T(8,128)S(1)} %bitcast.39), channel_id=1, replica_groups=mesh['zh'=2,'x'=4,'y'=4,'z'=8,'c'=2] {'y'}, dimensions={0} | all-to-all | bytes 4194304 | tf_op jit(solution)/shard_map/all_to_all | solution.py:23
  68.1 1.8 reduce_sum.18
  69.9 0.2 copy.25
  70.1 0.3 copy.19
  70.3 0.4 reshape.62
  70.8 33.6 %all_to_all.31 = f32[8,32,512]{2,1,0:T(8,128)S(1)} all-to-all(f32[8,32,512]{2,1,0:T(8,128)S(1)} %reshape.62), channel_id=1, replica_groups=mesh['zh'=2,'x'=4,'y'=4,'z'=8,'c'=2] {'z'}, dimensions={0} | all-to-all | bytes 1048576 | tf_op jit(solution)/shard_map/all_to_all | solution.py:23
  104.4 2.7 %collective-permute-start.2 = (f32[32,256]{1,0:T(8,128)S(1)}, f32[32,256]{1,0:T(8,128)S(1)}, u32[]{:S(2)}, u32[]{:S(2)}) collective-permute-start(f32[32,256]{1,0:T(8,128)S(1)} %get-tuple-element.22), channel_id=1, source_target_pairs={{64,0},{128,64},{192,128},{256,192},{320,256},{384,320},{448,384},... | collective-permute-start | bytes 98312 | tf_op jit(solution)/shard_map/ppermute | solution.py:34
  107.1 13.9 %collective-permute-start.1 = (f32[32,256]{1,0:T(8,128)S(1)}, f32[32,256]{1,0:T(8,128)S(1)}, u32[]{:S(2)}, u32[]{:S(2)}) collective-permute-start(f32[32,256]{1,0:T(8,128)S(1)} %get-tuple-element.23), channel_id=1, source_target_pairs={{0,64},{64,128},{128,192},{192,256},{256,320},{320,384},{384,448},... | collective-permute-start | bytes 98312 | tf_op jit(solution)/shard_map/ppermute | solution.py:34
  121.1 0.0 collective-permute-done.2
  121.1 1.6 collective-permute-done.1
  122.7 19.2 %all_to_all.32 = bf16[8,32,512]{2,1,0:T(8,128)(2,1)S(1)} all-to-all(bf16[8,32,512]{2,1,0:T(8,128)(2,1)S(1)} %broadcast_in_dim.64), channel_id=1, replica_groups=mesh['zh'=2,'x'=4,'y'=4,'z'=8,'c'=2] {'z'}, dimensions={0} | all-to-all | bytes 524288 | tf_op jit(solution)/shard_map/all_to_all | solution.py:23
  141.9 0.1 broadcast_in_dim.65
  142.0 13.3 %all_to_all.33.error_ref = bf16[4,8,32,512]{3,2,1,0:T(8,128)(2,1)S(1)} all-to-all(bf16[4,8,32,512]{3,2,1,0:T(8,128)(2,1)S(1)} %broadcast_in_dim.65), channel_id=1, replica_groups=mesh['zh'=2,'x'=4,'y'=4,'z'=8,'c'=2] {'y'}, dimensions={0} | all-to-all | bytes 2097152 | tf_op jit(solution)/shard_map/all_to_all | solution.py:23
  155.3 1.9 %collective-permute-start.3 = (bf16[4,8,32,512]{3,2,1,0:T(8,128)(2,1)S(1)}, bf16[4,8,32,512]{3,2,1,0:T(8,128)(2,1)}, u32[]{:S(2)}, u32[]{:S(2)}) collective-permute-start(bf16[4,8,32,512]{3,2,1,0:T(8,128)(2,1)S(1)} %all_to_all.33.error_ref), channel_id=1, source_target_pairs={{0,1},{1,0},{2,3},{3,2},{4,5},{5,4},{6,7},{7,6},{8,9},{9,8},{10,11... | collective-permute-start | bytes 3145736 | tf_op jit(solution)/shard_map/ppermute | solution.py:19
  157.2 3.8 %shard_map.77 = bf16[128,512]{1,0:T(8,128)(2,1)S(1)} custom-call(bf16[4,8,32,512]{3,2,1,0:T(8,128)(2,1)S(1)} %all_to_all.33.error_ref, bf16[256,4096]{1,0:T(8,128)(2,1)S(1)} %bitcast.36, bf16[256,4096]{1,0:T(8,128)(2,1)S(1)} %bitcast.37, bf16[256,4096]{1,0:T(8,128)(2,1)} %collective-permute-done.refs_2_.refs_3_, ...), custom_call_target="tpu_custom_call" | custom-call | flops 536870912 | bytes 5242880 | tf_op jit(solution)/shard_map/pallas_call | solution.py:73
  161.1 0.7 reshape.63
  161.8 0.0 collective-permute-done.3.other_ref
  161.8 9.9 %all-to-all-start.5 = ((bf16[32,4,512]{2,1,0:T(4,128)(2,1)}), bf16[32,4,512]{2,1,0:T(4,128)(2,1)S(1)}, u32[]{:S(2)}, u32[]{:S(2)}) async-start(bf16[32,4,512]{2,1,0:T(4,128)(2,1)} %reshape.63), calls=%async_computation.5 | async-start | bytes 262144 | tf_op jit(solution)/shard_map/all_to_all | solution.py:23
  171.7 0.1 copy.23
  171.8 2.1 %collective-permute-start.4 = (bf16[128,256]{0,1:T(8,128)(2,1)S(1)}, bf16[128,256]{0,1:T(8,128)(2,1)S(1)}, u32[]{:S(2)}, u32[]{:S(2)}) collective-permute-start(bf16[128,256]{0,1:T(8,128)(2,1)S(1)} %copy.23), channel_id=1, source_target_pairs={{0,1},{1,0},{2,3},{3,2},{4,5},{5,4},{6,7},{7,6},{8,9},{9,8},{10,11... | collective-permute-start | bytes 196616 | tf_op jit(solution)/shard_map/ppermute | solution.py:19
  173.9 0.1 copy.22
  174.1 0.9 collective-permute-done.4
  175.0 3.4 %shard_map.78 = bf16[2,256,2048]{2,1,0:T(8,128)(2,1)S(1)} custom-call(bf16[256,256]{1,0:T(8,128)(2,1)S(1)} %maximum_bitcast_fusion.feature_ref, bf16[4,8,32,512]{3,2,1,0:T(8,128)(2,1)S(1)} %all_to_all.33.error_ref, bf16[4,8,32,512]{3,2,1,0:T(8,128)(2,1)} %collective-permute-done.3.other_ref), custom_call_target="tpu_custom_call" | custom-call | flops 536870912 | bytes 4194304 | tf_op jit(solution)/shard_map/pallas_call | solution.py:103
  178.3 3.5 %copy.21 = bf16[1,256,2,2048]{3,2,1,0:T(2,128)(2,1)} copy(bf16[1,256,2,2048]{3,1,2,0:T(8,128)(2,1)S(1)} %bitcast.38) | data formatting | bytes 4194304
  181.8 4.8 %all-to-all-done.5 = bf16[32,4,512]{2,1,0:T(4,128)(2,1)S(1)} async-done(((bf16[32,4,512]{2,1,0:T(4,128)(2,1)}), bf16[32,4,512]{2,1,0:T(4,128)(2,1)S(1)}, u32[]{:S(2)}, u32[]{:S(2)}) %all-to-all-start.5) | async-done | bytes 131104 | tf_op jit(solution)/shard_map/all_to_all | solution.py:23
  186.6 0.1 reshape.64
  186.7 0.8 fusion.1
  (14 shorter events, 0.2 us)
Async XLA Ops:
  0.6 4.6 %copy-start = (bf16[1,4,32,128]{3,2,1,0:T(8,128)(2,1)S(1)}, bf16[1,4,32,128]{3,2,1,0:T(8,128)(2,1)}, u32[]{:S(2)}) copy-start(bf16[1,4,32,128]{3,2,1,0:T(8,128)(2,1)} %param.6) | copy-start | bytes 98308
  0.6 4.5 %copy-start.2 = (f32[1,16384]{1,0:T(1,128)S(1)}, f32[1,16384]{1,0:T(1,128)}, u32[]{:S(2)}) copy-start(f32[1,16384]{1,0:T(1,128)} %param.8) | copy-start | bytes 196612
  0.7 4.6 %copy-start.5 = (s32[1,4,32]{2,1,0:T(4,128)S(1)}, s32[1,4,32]{2,1,0:T(4,128)}, u32[]{:S(2)}) copy-start(s32[1,4,32]{2,1,0:T(4,128)} %param.7) | copy-start | bytes 1540
  0.7 21.6 %copy-start.3 = (bf16[1,4,2048]{2,1,0:T(4,128)(2,1)S(1)}, bf16[1,4,2048]{2,1,0:T(4,128)(2,1)}, u32[]{:S(2)}) copy-start(bf16[1,4,2048]{2,1,0:T(4,128)(2,1)} %param.11) | copy-start | bytes 49156
  0.7 21.6 %copy-start.4 = (f32[1,2048]{1,0:T(1,128)S(1)}, f32[1,2048]{1,0:T(1,128)}, u32[]{:S(2)}) copy-start(f32[1,2048]{1,0:T(1,128)} %param.10) | copy-start | bytes 24580
  3.2 34.3 %collective-permute-start = (bf16[256,4096]{1,0:T(8,128)(2,1)S(1)}, bf16[256,4096]{1,0:T(8,128)(2,1)}, u32[]{:S(2)}, u32[]{:S(2)}) collective-permute-start(bf16[256,4096]{1,0:T(8,128)(2,1)S(1)} %bitcast.34), channel_id=1, source_target_pairs={{0,1},{1,0},{2,3},{3,2},{4,5},{5,4},{6,7},{7,6},{8,9},{9,8},{10,11... | collective-permute-start | bytes 6291464 | tf_op jit(solution)/shard_map/ppermute | solution.py:19
  6.5 30.5 %all-to-all-start = ((bf16[32,4,512]{2,1,0:T(4,128)(2,1)}), bf16[32,4,512]{2,1,0:T(4,128)(2,1)S(1)}, u32[]{:S(2)}, u32[]{:S(2)}) async-start(bf16[32,4,512]{2,1,0:T(4,128)(2,1)} %bitcast.33), calls=%async_computation | async-start | bytes 262144 | tf_op jit(solution)/shard_map/all_to_all | solution.py:23
  37.0 1.6 copy-start.1
  104.4 16.7 %collective-permute-start.2 = (f32[32,256]{1,0:T(8,128)S(1)}, f32[32,256]{1,0:T(8,128)S(1)}, u32[]{:S(2)}, u32[]{:S(2)}) collective-permute-start(f32[32,256]{1,0:T(8,128)S(1)} %get-tuple-element.22), channel_id=1, source_target_pairs={{64,0},{128,64},{192,128},{256,192},{320,256},{384,320},{448,384},... | collective-permute-start | bytes 98312 | tf_op jit(solution)/shard_map/ppermute | solution.py:34
  107.1 15.5 %collective-permute-start.1 = (f32[32,256]{1,0:T(8,128)S(1)}, f32[32,256]{1,0:T(8,128)S(1)}, u32[]{:S(2)}, u32[]{:S(2)}) collective-permute-start(f32[32,256]{1,0:T(8,128)S(1)} %get-tuple-element.23), channel_id=1, source_target_pairs={{0,64},{64,128},{128,192},{192,256},{256,320},{320,384},{384,448},... | collective-permute-start | bytes 98312 | tf_op jit(solution)/shard_map/ppermute | solution.py:34
  155.3 6.5 %collective-permute-start.3 = (bf16[4,8,32,512]{3,2,1,0:T(8,128)(2,1)S(1)}, bf16[4,8,32,512]{3,2,1,0:T(8,128)(2,1)}, u32[]{:S(2)}, u32[]{:S(2)}) collective-permute-start(bf16[4,8,32,512]{3,2,1,0:T(8,128)(2,1)S(1)} %all_to_all.33.error_ref), channel_id=1, source_target_pairs={{0,1},{1,0},{2,3},{3,2},{4,5},{5,4},{6,7},{7,6},{8,9},{9,8},{10,11... | collective-permute-start | bytes 3145736 | tf_op jit(solution)/shard_map/ppermute | solution.py:19
  161.8 24.8 %all-to-all-start.5 = ((bf16[32,4,512]{2,1,0:T(4,128)(2,1)}), bf16[32,4,512]{2,1,0:T(4,128)(2,1)S(1)}, u32[]{:S(2)}, u32[]{:S(2)}) async-start(bf16[32,4,512]{2,1,0:T(4,128)(2,1)} %reshape.63), calls=%async_computation.5 | async-start | bytes 262144 | tf_op jit(solution)/shard_map/all_to_all | solution.py:23
  171.8 3.1 %collective-permute-start.4 = (bf16[128,256]{0,1:T(8,128)(2,1)S(1)}, bf16[128,256]{0,1:T(8,128)(2,1)S(1)}, u32[]{:S(2)}, u32[]{:S(2)}) collective-permute-start(bf16[128,256]{0,1:T(8,128)(2,1)S(1)} %copy.23), channel_id=1, source_target_pairs={{0,1},{1,0},{2,3},{3,2},{4,5},{5,4},{6,7},{7,6},{8,9},{9,8},{10,11... | collective-permute-start | bytes 196616 | tf_op jit(solution)/shard_map/ppermute | solution.py:19

commit v3 on v2

--- a/solution.py
+++ b/solution.py
@@ -11,8 +11,8 @@
 AXES = ("zh", "x", "y", "z", "c")
 SIZES = (2, 4, 4, 8, 2)
 SECTION, FEAT = ("zh", "x"), ("y", "z", "c")
-WIRE_Y = jnp.float32
-WIRE_Z = jnp.float32
+WIRE_Y = jnp.bfloat16
+WIRE_Z = jnp.bfloat16
 
 
 def swap_cores(block):
@@ -28,10 +28,17 @@
     return exchange(copies, axis)
 
 
-def to_layer(block, distance):
+def with_neighbours(mine, beyond):
     layers = SIZES[0] * SIZES[1]
-    route = [(i, i + distance) for i in range(layers) if 0 <= i + distance < layers]
-    return lax.ppermute(block, SECTION, route)
+    even = lax.axis_index(SECTION) % 2 == 0
+    rounds = []
+    for first, sent in ((0, jnp.where(even, beyond, mine)), (1, jnp.where(even, mine, beyond))):
+        route = []
+        for i in range(first, layers - 1, 2):
+            route += [(i, i + 1), (i + 1, i)]
+        rounds.append(lax.ppermute(sent, SECTION, route))
+    lower, upper = lax.optimization_barrier(tuple(rounds))
+    return jnp.where(even, upper, lower), jnp.where(even, lower, upper)
 
 
 def column_blocks(error_ref, col):
@@ -149,11 +156,13 @@
     part = part + jnp.where(here, shift[None], 0.0).reshape(part.shape)
     part = part.astype(WIRE_Y).reshape(ny, nz * tok, nc * width)
     part = jnp.sum(exchange(part, "y").astype(f32), axis=0)
+    f_swapped = swap_cores(f_other)
+    part, f_swapped = lax.optimization_barrier((part, f_swapped))
     part = part.reshape(nz * tok, nc, nz, col).transpose(2, 0, 1, 3).astype(WIRE_Z)
     part = jnp.sum(exchange(part.reshape(nz, nz * tok, nc * col), "z").astype(f32), axis=0)
 
     mine, beyond = part[:, :col], part[:, col:]
-    got, got_next = lax.optimization_barrier((to_layer(beyond, 1), to_layer(mine, -1)))
+    got, got_next = with_neighbours(mine, beyond)
     error_next = jnp.where(layer == last_layer, 0.0, beyond + got_next)
     error = jnp.concatenate([mine + got, error_next], axis=1).astype(bf16)
 
@@ -164,7 +173,7 @@
     grad, error_other = lax.optimization_barrier((grad, error_other))
     returned = exchange(grad, ("y", "z"))
 
-    f_own = jnp.concatenate([f_mine, swap_cores(f_other)], axis=0).T
+    f_own = jnp.concatenate([f_mine, f_swapped], axis=0).T
     grad_decoder = decoder_grads(f_own, error, error_other).transpose(1, 0, 2)[None]
 
     table = returned.transpose(1, 0, 2).reshape(tok, blocks, BLK)

time: 188 us -> 165 us (0.88)
  blocking collectives: 93.3 us -> 33.3 us
  waiting for transfers between devices: 17.2 us -> 50.6 us
  starting transfers between devices: 48.1 us -> 51.2 us
    all_to_all x4 -> x2, blocking collectives: 93.3 us -> 33.3 us  [exchange(): return lax.all_to_all(block, axis, split_axis=0, concat_axis=0, tiled=True)]
    all_to_all x2 -> x4, waiting for transfers between devices: 14.7 us -> 44.1 us  [exchange(): return lax.all_to_all(block, axis, split_axis=0, concat_axis=0, tiled=True)]
    all_to_all x2 -> x4, starting transfers between devices: 25.4 us -> 35.4 us  [exchange(): return lax.all_to_all(block, axis, split_axis=0, concat_axis=0, tiled=True)]
    ppermute x2, starting transfers between devices: 16.7 us -> 10.1 us  [with_neighbours(): rounds.append(lax.ppermute(sent, SECTION, route))]
    ppermute x2, waiting for transfers between devices: 1.56 us -> 6.56 us  [with_neighbours(): rounds.append(lax.ppermute(sent, SECTION, route))]
  transfers between devices with their start and end apart: 7 -> 9, of which waited for: 4 -> 5; matrix products, arithmetic and copies ran while one was open for 6% -> 7% of each run, Pallas kernels for 4% -> 4%
where the time goes in v3:
time: 165 us; the launch traced here: 164 us
  starting transfers between devices  51.2 us (31%)
  waiting for transfers between devices  50.6 us (31%)
  blocking collectives  33.3 us (20%)
  local copies, waits for them, and re-layouts  15.3 us (9%)
  Pallas kernels  7.21 us (4%)
  matrix products  4.79 us (3%)
    all_to_all x4, waiting for transfers between devices, exchange(): return lax.all_to_all(block, axis, split_axis=0, concat_axis=0, tiled=True)  44.1 us
    all_to_all x4, starting transfers between devices, exchange(): return lax.all_to_all(block, axis, split_axis=0, concat_axis=0, tiled=True)  35.4 us
    all_to_all x2, blocking collectives, exchange(): return lax.all_to_all(block, axis, split_axis=0, concat_axis=0, tiled=True)  33.3 us
    ppermute x2, starting transfers between devices, with_neighbours(): rounds.append(lax.ppermute(sent, SECTION, route))  10.1 us
    unnamed x18, local copies, waits for them, and re-layouts  7.44 us
    ppermute x2, waiting for transfers between devices, with_neighbours(): rounds.append(lax.ppermute(sent, SECTION, route))  6.56 us
    ppermute x3, starting transfers between devices, swap_cores(): return lax.ppermute(block, 'c', [(0, 1), (1, 0)])  5.75 us
    broadcast_in_dim x4, local copies, waits for them, and re-layouts, per_device(): part = part + jnp.where(here, shift[None], 0.0).reshape(part.shape)  4.94 us
  transfers between devices with their start and end apart: 9, of which 5 were waited for; matrix products, arithmetic and copies ran while one was open for 7% of the time, Pallas kernels for 4%

profile of v3, /device:TPU:6, one launch (start us, length us, event | category | flops | bytes accessed | tf_op | source)
XLA Modules:
  0.0 163.7 jit_solution(11498097632668243547)
XLA Ops:
  0.6 0.0 copy-start
  0.6 0.0 copy-start.2
  0.7 0.0 copy-start.5
  0.7 0.0 copy-start.3
  0.7 0.0 copy-start.4
  0.7 2.5 %copy.24 = bf16[32,8,2,2048]{3,1,2,0:T(8,128)(2,1)S(1)} copy(bf16[32,8,2,2048]{3,2,1,0:T(2,128)(2,1)} %bitcast.40) | data formatting | bytes 4194304
  3.2 1.9 %collective-permute-start = (bf16[256,4096]{1,0:T(8,128)(2,1)S(1)}, bf16[256,4096]{1,0:T(8,128)(2,1)}, u32[]{:S(2)}, u32[]{:S(2)}) collective-permute-start(bf16[256,4096]{1,0:T(8,128)(2,1)S(1)} %bitcast.34), channel_id=1, source_target_pairs={{0,1},{1,0},{2,3},{3,2},{4,5},{5,4},{6,7},{7,6},{8,9},{9,8},{10,11... | collective-permute-start | bytes 6291464 | tf_op jit(solution)/shard_map/ppermute | solution.py:19
  5.2 0.0 copy-done.2
  5.2 0.0 copy-done
  5.2 0.0 copy-done.5
  5.2 0.3 fusion.11
  5.6 0.1 fusion.12
  5.7 0.1 reshape.57
  5.8 0.8 copy.27
  6.5 15.5 %all-to-all-start = ((bf16[32,4,512]{2,1,0:T(4,128)(2,1)}), bf16[32,4,512]{2,1,0:T(4,128)(2,1)S(1)}, u32[]{:S(2)}, u32[]{:S(2)}) async-start(bf16[32,4,512]{2,1,0:T(4,128)(2,1)} %bitcast.33), calls=%async_computation | async-start | bytes 262144 | tf_op jit(solution)/shard_map/all_to_all | solution.py:23
  22.1 0.1 broadcast_in_dim.57
  22.2 0.1 broadcast_in_dim.58
  22.3 0.0 copy-done.3
  22.3 0.0 copy-done.4
  22.3 1.8 %broadcast_in_dim.60 = f32[32,4,4096]{2,1,0:T(4,128)} broadcast(f32[4,4096]{1,0:T(4,128)S(1)} %concatenate.14), dimensions={1,2} | broadcast | bytes 2162688 | tf_op jit(solution)/shard_map/jit(_where)/broadcast_in_dim | solution.py:156
  24.1 3.0 %broadcast_in_dim.61 = f32[128,4096]{1,0:T(8,128)} reshape(f32[32,4,4096]{2,1,0:T(4,128)} %broadcast_in_dim.60) | data formatting | bytes 4194304 | tf_op jit(solution)/shard_map/jit(_where)/broadcast_in_dim | solution.py:156
  27.1 9.9 %all-to-all-done = bf16[32,4,512]{2,1,0:T(4,128)(2,1)S(1)} async-done(((bf16[32,4,512]{2,1,0:T(4,128)(2,1)}), bf16[32,4,512]{2,1,0:T(4,128)(2,1)S(1)}, u32[]{:S(2)}, u32[]{:S(2)}) %all-to-all-start) | async-done | bytes 131104 | tf_op jit(solution)/shard_map/all_to_all | solution.py:23
  37.0 0.0 copy-start.1
  37.1 0.4 fusion.23
  37.5 0.0 collective-permute-done.refs_2_.refs_3_
  37.5 1.1 copy-done.1
  38.6 3.2 %fusion.1 = bf16[128,4096]{1,0:T(8,128)(2,1)} fusion(f32[128,4096]{1,0:T(8,128)S(1)} %fusion.23, bf16[256,4096]{1,0:T(8,128)(2,1)} %collective-permute-done.refs_2_.refs_3_, f32[128,4096]{1,0:T(8,128)S(1)} %copy-done.1, pred[128]{0:T(512)(128)(4,1)S(1)} %broadcast_in_dim.58, bf16[128,512]{1,0:T(8,128)(2,1)S(1)} %reshape.58), kind=kOutput, calls=%fused_computation.2 | convolution fusion | flops 270532608 | bytes 7406080 | tf_op jit(solution)/shard_map/dot_general | solution.py:152
  41.8 3.5 %all-to-all-start.1 = ((bf16[4,32,4096]{2,1,0:T(8,128)(2,1)}), bf16[4,32,4096]{2,1,0:T(8,128)(2,1)S(1)}, u32[]{:S(2)}, u32[]{:S(2)}) async-start(bf16[4,32,4096]{2,1,0:T(8,128)(2,1)} %bitcast.39), calls=%async_computation.1 | async-start | bytes 2097152 | tf_op jit(solution)/shard_map/all_to_all | solution.py:23
  45.4 0.1 copy.23
  45.5 1.9 %collective-permute-start.1 = (bf16[128,256]{0,1:T(8,128)(2,1)S(1)}, bf16[128,256]{0,1:T(8,128)(2,1)S(1)}, u32[]{:S(2)}, u32[]{:S(2)}) collective-permute-start(bf16[128,256]{0,1:T(8,128)(2,1)S(1)} %copy.23), channel_id=1, source_target_pairs={{0,1},{1,0},{2,3},{3,2},{4,5},{5,4},{6,7},{7,6},{8,9},{9,8},{10,11... | collective-permute-start | bytes 196616 | tf_op jit(solution)/shard_map/ppermute | solution.py:19
  47.4 10.6 %all-to-all-done.1 = bf16[4,32,4096]{2,1,0:T(8,128)(2,1)S(1)} async-done(((bf16[4,32,4096]{2,1,0:T(8,128)(2,1)}), bf16[4,32,4096]{2,1,0:T(8,128)(2,1)S(1)}, u32[]{:S(2)}, u32[]{:S(2)}) %all-to-all-start.1) | async-done | bytes 1048608 | tf_op jit(solution)/shard_map/all_to_all | solution.py:23
  58.0 0.1 convert_reduce_fusion
  58.1 0.0 collective-permute-done.1
  58.2 0.2 copy.19
  58.4 0.9 reshape.60
  59.3 6.4 %all-to-all-start.2 = ((bf16[8,32,512]{2,1,0:T(8,128)(2,1)}), bf16[8,32,512]{2,1,0:T(8,128)(2,1)S(1)}, u32[]{:S(2)}, u32[]{:S(2)}) async-start(bf16[8,32,512]{2,1,0:T(8,128)(2,1)} %reshape.60), calls=%async_computation.2 | async-start | bytes 524288 | tf_op jit(solution)/shard_map/all_to_all | solution.py:23
  65.7 15.7 %all-to-all-done.2 = bf16[8,32,512]{2,1,0:T(8,128)(2,1)S(1)} async-done(((bf16[8,32,512]{2,1,0:T(8,128)(2,1)}), bf16[8,32,512]{2,1,0:T(8,128)(2,1)S(1)}, u32[]{:S(2)}, u32[]{:S(2)}) %all-to-all-start.2) | async-done | bytes 262176 | tf_op jit(solution)/shard_map/all_to_all | solution.py:23
  81.4 8.1 %collective-permute-start.3 = (f32[32,256]{1,0:T(8,128)S(1)}, f32[32,256]{1,0:T(8,128)S(1)}, u32[]{:S(2)}, u32[]{:S(2)}) collective-permute-start(f32[32,256]{1,0:T(8,128)S(1)} %get-tuple-element.26), channel_id=1, source_target_pairs={{64,128},{128,64},{192,256},{256,192},{320,384},{384,320},{65,129}... | collective-permute-start | bytes 98312 | tf_op jit(solution)/shard_map/ppermute | solution.py:39
  89.5 1.9 %collective-permute-start.2 = (f32[32,256]{1,0:T(8,128)S(1)}, f32[32,256]{1,0:T(8,128)S(1)}, u32[]{:S(2)}, u32[]{:S(2)}) collective-permute-start(f32[32,256]{1,0:T(8,128)S(1)} %get-tuple-element.27), channel_id=1, source_target_pairs={{0,64},{64,0},{128,192},{192,128},{256,320},{320,256},{384,448},{4... | collective-permute-start | bytes 98312 | tf_op jit(solution)/shard_map/ppermute | solution.py:39
  91.5 6.6 %collective-permute-done.3 = f32[32,256]{1,0:T(8,128)S(1)} collective-permute-done((f32[32,256]{1,0:T(8,128)S(1)}, f32[32,256]{1,0:T(8,128)S(1)}, u32[]{:S(2)}, u32[]{:S(2)}) %collective-permute-start.3) | collective-permute-done | bytes 32800 | tf_op jit(solution)/shard_map/ppermute | solution.py:39
  98.0 0.0 collective-permute-done.2
  98.1 20.0 %all_to_all.30 = bf16[8,32,512]{2,1,0:T(8,128)(2,1)S(1)} all-to-all(bf16[8,32,512]{2,1,0:T(8,128)(2,1)S(1)} %broadcast_in_dim.64), channel_id=1, replica_groups=mesh['zh'=2,'x'=4,'y'=4,'z'=8,'c'=2] {'z'}, dimensions={0} | all-to-all | bytes 524288 | tf_op jit(solution)/shard_map/all_to_all | solution.py:23
  118.1 0.1 broadcast_in_dim.65
  118.2 13.3 %all_to_all.31.error_ref = bf16[4,8,32,512]{3,2,1,0:T(8,128)(2,1)S(1)} all-to-all(bf16[4,8,32,512]{3,2,1,0:T(8,128)(2,1)S(1)} %broadcast_in_dim.65), channel_id=1, replica_groups=mesh['zh'=2,'x'=4,'y'=4,'z'=8,'c'=2] {'y'}, dimensions={0} | all-to-all | bytes 2097152 | tf_op jit(solution)/shard_map/all_to_all | solution.py:23
  131.5 1.9 %collective-permute-start.4 = (bf16[4,8,32,512]{3,2,1,0:T(8,128)(2,1)S(1)}, bf16[4,8,32,512]{3,2,1,0:T(8,128)(2,1)}, u32[]{:S(2)}, u32[]{:S(2)}) collective-permute-start(bf16[4,8,32,512]{3,2,1,0:T(8,128)(2,1)S(1)} %all_to_all.31.error_ref), channel_id=1, source_target_pairs={{0,1},{1,0},{2,3},{3,2},{4,5},{5,4},{6,7},{7,6},{8,9},{9,8},{10,11... | collective-permute-start | bytes 3145736 | tf_op jit(solution)/shard_map/ppermute | solution.py:19
  133.4 3.8 %shard_map.77 = bf16[128,512]{1,0:T(8,128)(2,1)S(1)} custom-call(bf16[4,8,32,512]{3,2,1,0:T(8,128)(2,1)S(1)} %all_to_all.31.error_ref, bf16[256,4096]{1,0:T(8,128)(2,1)S(1)} %bitcast.36, bf16[256,4096]{1,0:T(8,128)(2,1)S(1)} %bitcast.37, bf16[256,4096]{1,0:T(8,128)(2,1)} %collective-permute-done.refs_2_.refs_3_, ...), custom_call_target="tpu_custom_call" | custom-call | flops 536870912 | bytes 5242880 | tf_op jit(solution)/shard_map/pallas_call | solution.py:80
  137.3 0.7 reshape.61
  137.9 0.0 collective-permute-done.4.other_ref
  137.9 9.9 %all-to-all-start.5 = ((bf16[32,4,512]{2,1,0:T(4,128)(2,1)}), bf16[32,4,512]{2,1,0:T(4,128)(2,1)S(1)}, u32[]{:S(2)}, u32[]{:S(2)}) async-start(bf16[32,4,512]{2,1,0:T(4,128)(2,1)} %reshape.61), calls=%async_computation.5 | async-start | bytes 262144 | tf_op jit(solution)/shard_map/all_to_all | solution.py:23
  147.9 0.1 copy.22
  148.0 3.4 %shard_map.78 = bf16[2,256,2048]{2,1,0:T(8,128)(2,1)S(1)} custom-call(bf16[256,256]{1,0:T(8,128)(2,1)S(1)} %maximum_bitcast_fusion.feature_ref, bf16[4,8,32,512]{3,2,1,0:T(8,128)(2,1)S(1)} %all_to_all.31.error_ref, bf16[4,8,32,512]{3,2,1,0:T(8,128)(2,1)} %collective-permute-done.4.other_ref), custom_call_target="tpu_custom_call" | custom-call | flops 536870912 | bytes 4194304 | tf_op jit(solution)/shard_map/pallas_call | solution.py:110
  151.4 3.5 %copy.21 = bf16[1,256,2,2048]{3,2,1,0:T(2,128)(2,1)} copy(bf16[1,256,2,2048]{3,1,2,0:T(8,128)(2,1)S(1)} %bitcast.38) | data formatting | bytes 4194304
  154.8 7.9 %all-to-all-done.5 = bf16[32,4,512]{2,1,0:T(4,128)(2,1)S(1)} async-done(((bf16[32,4,512]{2,1,0:T(4,128)(2,1)}), bf16[32,4,512]{2,1,0:T(4,128)(2,1)S(1)}, u32[]{:S(2)}, u32[]{:S(2)}) %all-to-all-start.5) | async-done | bytes 131104 | tf_op jit(solution)/shard_map/all_to_all | solution.py:23
  162.8 0.1 reshape.62
  162.9 0.8 fusion.2
  (15 shorter events, 0.3 us)
Async XLA Ops:
  0.6 4.6 %copy-start = (bf16[1,4,32,128]{3,2,1,0:T(8,128)(2,1)S(1)}, bf16[1,4,32,128]{3,2,1,0:T(8,128)(2,1)}, u32[]{:S(2)}) copy-start(bf16[1,4,32,128]{3,2,1,0:T(8,128)(2,1)} %param.6) | copy-start | bytes 98308
  0.6 4.5 %copy-start.2 = (f32[1,16384]{1,0:T(1,128)S(1)}, f32[1,16384]{1,0:T(1,128)}, u32[]{:S(2)}) copy-start(f32[1,16384]{1,0:T(1,128)} %param.8) | copy-start | bytes 196612
  0.7 4.6 %copy-start.5 = (s32[1,4,32]{2,1,0:T(4,128)S(1)}, s32[1,4,32]{2,1,0:T(4,128)}, u32[]{:S(2)}) copy-start(s32[1,4,32]{2,1,0:T(4,128)} %param.7) | copy-start | bytes 1540
  0.7 21.6 %copy-start.3 = (bf16[1,4,2048]{2,1,0:T(4,128)(2,1)S(1)}, bf16[1,4,2048]{2,1,0:T(4,128)(2,1)}, u32[]{:S(2)}) copy-start(bf16[1,4,2048]{2,1,0:T(4,128)(2,1)} %param.11) | copy-start | bytes 49156
  0.7 21.6 %copy-start.4 = (f32[1,2048]{1,0:T(1,128)S(1)}, f32[1,2048]{1,0:T(1,128)}, u32[]{:S(2)}) copy-start(f32[1,2048]{1,0:T(1,128)} %param.10) | copy-start | bytes 24580
  3.2 34.3 %collective-permute-start = (bf16[256,4096]{1,0:T(8,128)(2,1)S(1)}, bf16[256,4096]{1,0:T(8,128)(2,1)}, u32[]{:S(2)}, u32[]{:S(2)}) collective-permute-start(bf16[256,4096]{1,0:T(8,128)(2,1)S(1)} %bitcast.34), channel_id=1, source_target_pairs={{0,1},{1,0},{2,3},{3,2},{4,5},{5,4},{6,7},{7,6},{8,9},{9,8},{10,11... | collective-permute-start | bytes 6291464 | tf_op jit(solution)/shard_map/ppermute | solution.py:19
  6.5 30.5 %all-to-all-start = ((bf16[32,4,512]{2,1,0:T(4,128)(2,1)}), bf16[32,4,512]{2,1,0:T(4,128)(2,1)S(1)}, u32[]{:S(2)}, u32[]{:S(2)}) async-start(bf16[32,4,512]{2,1,0:T(4,128)(2,1)} %bitcast.33), calls=%async_computation | async-start | bytes 262144 | tf_op jit(solution)/shard_map/all_to_all | solution.py:23
  37.0 1.6 copy-start.1
  41.8 16.1 %all-to-all-start.1 = ((bf16[4,32,4096]{2,1,0:T(8,128)(2,1)}), bf16[4,32,4096]{2,1,0:T(8,128)(2,1)S(1)}, u32[]{:S(2)}, u32[]{:S(2)}) async-start(bf16[4,32,4096]{2,1,0:T(8,128)(2,1)} %bitcast.39), calls=%async_computation.1 | async-start | bytes 2097152 | tf_op jit(solution)/shard_map/all_to_all | solution.py:23
  45.5 12.6 %collective-permute-start.1 = (bf16[128,256]{0,1:T(8,128)(2,1)S(1)}, bf16[128,256]{0,1:T(8,128)(2,1)S(1)}, u32[]{:S(2)}, u32[]{:S(2)}) collective-permute-start(bf16[128,256]{0,1:T(8,128)(2,1)S(1)} %copy.23), channel_id=1, source_target_pairs={{0,1},{1,0},{2,3},{3,2},{4,5},{5,4},{6,7},{7,6},{8,9},{9,8},{10,11... | collective-permute-start | bytes 196616 | tf_op jit(solution)/shard_map/ppermute | solution.py:19
  59.3 22.1 %all-to-all-start.2 = ((bf16[8,32,512]{2,1,0:T(8,128)(2,1)}), bf16[8,32,512]{2,1,0:T(8,128)(2,1)S(1)}, u32[]{:S(2)}, u32[]{:S(2)}) async-start(bf16[8,32,512]{2,1,0:T(8,128)(2,1)} %reshape.60), calls=%async_computation.2 | async-start | bytes 524288 | tf_op jit(solution)/shard_map/all_to_all | solution.py:23
  81.4 16.6 %collective-permute-start.3 = (f32[32,256]{1,0:T(8,128)S(1)}, f32[32,256]{1,0:T(8,128)S(1)}, u32[]{:S(2)}, u32[]{:S(2)}) collective-permute-start(f32[32,256]{1,0:T(8,128)S(1)} %get-tuple-element.26), channel_id=1, source_target_pairs={{64,128},{128,64},{192,256},{256,192},{320,384},{384,320},{65,129}... | collective-permute-start | bytes 98312 | tf_op jit(solution)/shard_map/ppermute | solution.py:39
  89.5 8.5 %collective-permute-start.2 = (f32[32,256]{1,0:T(8,128)S(1)}, f32[32,256]{1,0:T(8,128)S(1)}, u32[]{:S(2)}, u32[]{:S(2)}) collective-permute-start(f32[32,256]{1,0:T(8,128)S(1)} %get-tuple-element.27), channel_id=1, source_target_pairs={{0,64},{64,0},{128,192},{192,128},{256,320},{320,256},{384,448},{4... | collective-permute-start | bytes 98312 | tf_op jit(solution)/shard_map/ppermute | solution.py:39
  131.5 6.5 %collective-permute-start.4 = (bf16[4,8,32,512]{3,2,1,0:T(8,128)(2,1)S(1)}, bf16[4,8,32,512]{3,2,1,0:T(8,128)(2,1)}, u32[]{:S(2)}, u32[]{:S(2)}) collective-permute-start(bf16[4,8,32,512]{3,2,1,0:T(8,128)(2,1)S(1)} %all_to_all.31.error_ref), channel_id=1, source_target_pairs={{0,1},{1,0},{2,3},{3,2},{4,5},{5,4},{6,7},{7,6},{8,9},{9,8},{10,11... | collective-permute-start | bytes 3145736 | tf_op jit(solution)/shard_map/ppermute | solution.py:19
  137.9 24.8 %all-to-all-start.5 = ((bf16[32,4,512]{2,1,0:T(4,128)(2,1)}), bf16[32,4,512]{2,1,0:T(4,128)(2,1)S(1)}, u32[]{:S(2)}, u32[]{:S(2)}) async-start(bf16[32,4,512]{2,1,0:T(4,128)(2,1)} %reshape.61), calls=%async_computation.5 | async-start | bytes 262144 | tf_op jit(solution)/shard_map/all_to_all | solution.py:23

commit v4 on v3

--- a/solution.py
+++ b/solution.py
@@ -29,14 +29,17 @@
 
 
 def with_neighbours(mine, beyond):
-    layers = SIZES[0] * SIZES[1]
+    layers, nz = SIZES[0] * SIZES[1], SIZES[3]
     even = lax.axis_index(SECTION) % 2 == 0
     rounds = []
     for first, sent in ((0, jnp.where(even, beyond, mine)), (1, jnp.where(even, mine, beyond))):
         route = []
         for i in range(first, layers - 1, 2):
-            route += [(i, i + 1), (i + 1, i)]
-        rounds.append(lax.ppermute(sent, SECTION, route))
+            far = (i + 1) % SIZES[1] == 0
+            for z in range(nz):
+                here, there = i * nz + z, (i + 1) * nz + (nz - 1 - z if far else z)
+                route += [(here, there), (there, here)]
+        rounds.append(lax.ppermute(sent, SECTION + ("z",), route))
     lower, upper = lax.optimization_barrier(tuple(rounds))
     return jnp.where(even, upper, lower), jnp.where(even, lower, upper)
 
@@ -124,7 +127,6 @@
     bf16, f32 = jnp.bfloat16, jnp.float32
     ny, nz, nc = SIZES[2:]
     core = lax.axis_index("c")
-    chip = lax.axis_index(("y", "z"))
     layer = lax.axis_index(SECTION)
     last_layer = SIZES[0] * SIZES[1] - 1
     tiles, ids = pre_tiles[0], block_ids[0]
@@ -150,23 +152,28 @@
 
     part = jnp.dot(f_mine, weights, preferred_element_type=f32)
     part = part + jnp.dot(f_other, weights_other, preferred_element_type=f32)
+    part = part.astype(WIRE_Y).reshape(ny, nz * tok, nc * width)
+    part = jnp.sum(exchange(part, "y").astype(f32), axis=0)
     shift = dec_bias[0][None, :] - targets[0].astype(f32)
     shift = jnp.concatenate([shift, jnp.zeros_like(shift)], axis=1)
-    here = jnp.arange(ny * nz)[:, None, None] == chip
+    here = jnp.arange(nz)[:, None, None] == lax.axis_index("z")
     part = part + jnp.where(here, shift[None], 0.0).reshape(part.shape)
-    part = part.astype(WIRE_Y).reshape(ny, nz * tok, nc * width)
-    part = jnp.sum(exchange(part, "y").astype(f32), axis=0)
     f_swapped = swap_cores(f_other)
     part, f_swapped = lax.optimization_barrier((part, f_swapped))
+    mirrored = lax.axis_index("zh") % 2 == 1
     part = part.reshape(nz * tok, nc, nz, col).transpose(2, 0, 1, 3).astype(WIRE_Z)
-    part = jnp.sum(exchange(part.reshape(nz, nz * tok, nc * col), "z").astype(f32), axis=0)
+    part = part.reshape(nz, nz * tok, nc * col)
+    part = jnp.where(mirrored, part[::-1], part)
+    part = jnp.sum(exchange(part, "z").astype(f32), axis=0)
 
     mine, beyond = part[:, :col], part[:, col:]
     got, got_next = with_neighbours(mine, beyond)
     error_next = jnp.where(layer == last_layer, 0.0, beyond + got_next)
     error = jnp.concatenate([mine + got, error_next], axis=1).astype(bf16)
 
-    error = gather(gather(error, "z"), "y").reshape(ny, nz, nz * tok, nc * col)
+    error = gather(error, "z").reshape(nz, nz * tok, nc * col)
+    error = jnp.where(mirrored, error[::-1], error)
+    error = gather(error, "y")
     error_other = swap_cores(error)
 
     grad = feature_grads(error, weights, weights_other).reshape(ny * nz, tok, -1)

time: 165 us -> 160 us (0.970)
  starting transfers between devices: 51.2 us -> 46.6 us
  local copies, waits for them, and re-layouts: 15.3 us -> 11.5 us
  blocking collectives: 33.3 us -> 35.6 us
  other arithmetic: 0.36 us -> 2.33 us
    ppermute x2, starting transfers between devices: 10.1 us -> 7.25 us  [with_neighbours(): rounds.append(lax.ppermute(sent, SECTION + ('z',), route))]
    all_to_all x2, blocking collectives: 33.3 us -> 35.6 us  [exchange(): return lax.all_to_all(block, axis, split_axis=0, concat_axis=0, tiled=True)]
    ppermute x2, waiting for transfers between devices: 6.56 us -> 4.58 us  [with_neighbours(): rounds.append(lax.ppermute(sent, SECTION + ('z',), route))]
    all_to_all x4, waiting for transfers between devices: 44.1 us -> 46 us  [exchange(): return lax.all_to_all(block, axis, split_axis=0, concat_axis=0, tiled=True)]
    broadcast_in_dim x4, local copies, waits for them, and re-layouts: 4.94 us -> 3.05 us  [per_device(): part = part + jnp.where(here, shift[None], 0.0).reshape(part.shape)]
    all_to_all x4, starting transfers between devices: 35.4 us -> 33.6 us  [exchange(): return lax.all_to_all(block, axis, split_axis=0, concat_axis=0, tiled=True)]
    unnamed x18 -> x16, local copies, waits for them, and re-layouts: 7.44 us -> 6.3 us
  transfers between devices with their start and end apart: 9 -> 9, of which waited for: 5 -> 5; matrix products, arithmetic and copies ran while one was open for 7% -> 7% of each run, Pallas kernels for 4% -> 5%
where the time goes in v4:
time: 160 us
  waiting for transfers between devices  50.6 us (32%)
  starting transfers between devices  46.6 us (29%)
  blocking collectives  35.6 us (22%)
  local copies, waits for them, and re-layouts  11.5 us (7%)
  Pallas kernels  7.21 us (5%)
  matrix products  4.68 us (3%)
  other arithmetic  2.33 us (1%)
    all_to_all x4, waiting for transfers between devices, exchange(): return lax.all_to_all(block, axis, split_axis=0, concat_axis=0, tiled=True)  46 us
    all_to_all x2, blocking collectives, exchange(): return lax.all_to_all(block, axis, split_axis=0, concat_axis=0, tiled=True)  35.6 us
    all_to_all x4, starting transfers between devices, exchange(): return lax.all_to_all(block, axis, split_axis=0, concat_axis=0, tiled=True)  33.6 us
    ppermute x2, starting transfers between devices, with_neighbours(): rounds.append(lax.ppermute(sent, SECTION + ('z',), route))  7.25 us
    unnamed x16, local copies, waits for them, and re-layouts  6.3 us
    ppermute x3, starting transfers between devices, swap_cores(): return lax.ppermute(block, 'c', [(0, 1), (1, 0)])  5.75 us
    ppermute x2, waiting for transfers between devices, with_neighbours(): rounds.append(lax.ppermute(sent, SECTION + ('z',), route))  4.58 us
    pallas_call x1, Pallas kernels, feature_grads(): pl.pallas_call(functools.partial(grad_kernel, both // 2), grid=(steps,),...  3.85 us
  transfers between devices with their start and end apart: 9, of which 5 were waited for; matrix products, arithmetic and copies ran while one was open for 7% of the time, Pallas kernels for 5%

profile of v4, /device:TPU:6, one launch (start us, length us, event | category | flops | bytes accessed | tf_op | source)
XLA Modules:
  0.0 159.5 jit_solution(9093289803119151493)
XLA Ops:
  0.6 0.0 copy-start
  0.6 0.0 copy-start.1
  0.7 0.0 copy-start.4
  0.7 2.5 %copy.24 = bf16[32,8,2,2048]{3,1,2,0:T(8,128)(2,1)S(1)} copy(bf16[32,8,2,2048]{3,2,1,0:T(2,128)(2,1)} %bitcast.40) | data formatting | bytes 4194304
  3.2 1.9 %collective-permute-start = (bf16[256,4096]{1,0:T(8,128)(2,1)S(1)}, bf16[256,4096]{1,0:T(8,128)(2,1)}, u32[]{:S(2)}, u32[]{:S(2)}) collective-permute-start(bf16[256,4096]{1,0:T(8,128)(2,1)S(1)} %bitcast.34), channel_id=1, source_target_pairs={{0,1},{1,0},{2,3},{3,2},{4,5},{5,4},{6,7},{7,6},{8,9},{9,8},{10,11... | collective-permute-start | bytes 6291464 | tf_op jit(solution)/shard_map/ppermute | solution.py:19
  5.1 0.0 copy-done.1
  5.2 0.0 copy-done
  5.2 0.0 copy-done.4
  5.2 0.3 fusion.10
  5.5 0.1 fusion.11
  5.6 0.1 reshape.57
  5.7 0.8 copy.27
  6.5 15.5 %all-to-all-start = ((bf16[32,4,512]{2,1,0:T(4,128)(2,1)}), bf16[32,4,512]{2,1,0:T(4,128)(2,1)S(1)}, u32[]{:S(2)}, u32[]{:S(2)}) async-start(bf16[32,4,512]{2,1,0:T(4,128)(2,1)} %bitcast.33), calls=%async_computation | async-start | bytes 262144 | tf_op jit(solution)/shard_map/all_to_all | solution.py:23
  22.0 14.9 %all-to-all-done = bf16[32,4,512]{2,1,0:T(4,128)(2,1)S(1)} async-done(((bf16[32,4,512]{2,1,0:T(4,128)(2,1)}), bf16[32,4,512]{2,1,0:T(4,128)(2,1)S(1)}, u32[]{:S(2)}, u32[]{:S(2)}) %all-to-all-start) | async-done | bytes 131104 | tf_op jit(solution)/shard_map/all_to_all | solution.py:23
  37.0 0.4 fusion.22
  37.5 0.0 collective-permute-done.refs_2_.refs_3_
  37.5 3.1 %fusion = bf16[128,4096]{1,0:T(8,128)(2,1)} fusion(f32[128,4096]{1,0:T(8,128)S(1)} %fusion.22, bf16[256,4096]{1,0:T(8,128)(2,1)} %collective-permute-done.refs_2_.refs_3_, bf16[128,512]{1,0:T(8,128)(2,1)S(1)} %reshape.58), kind=kOutput, calls=%fused_computation.1 | convolution fusion | flops 269484032 | bytes 5308416 | tf_op jit(solution)/shard_map/dot_general | solution.py:154
  40.5 0.0 copy-start.2
  40.6 0.0 copy-start.3
  40.6 3.6 %all-to-all-start.1 = ((bf16[4,32,4096]{2,1,0:T(8,128)(2,1)}), bf16[4,32,4096]{2,1,0:T(8,128)(2,1)S(1)}, u32[]{:S(2)}, u32[]{:S(2)}) async-start(bf16[4,32,4096]{2,1,0:T(8,128)(2,1)} %bitcast.39), calls=%async_computation.1 | async-start | bytes 2097152 | tf_op jit(solution)/shard_map/all_to_all | solution.py:23
  44.2 0.0 copy-done.2
  44.2 0.0 copy-done.3
  44.3 0.9 broadcast_in_dim.60
  45.1 2.0 %broadcast_in_dim.61 = f32[32,4096]{1,0:T(8,128)} reshape(f32[8,4,4096]{2,1,0:T(4,128)} %broadcast_in_dim.60) | data formatting | bytes 1048576 | tf_op jit(solution)/shard_map/jit(_where)/broadcast_in_dim | solution.py:160
  47.2 0.1 broadcast_in_dim.57
  47.2 0.1 broadcast_in_dim.58
  47.3 0.1 copy.23
  47.5 1.9 %collective-permute-start.1 = (bf16[128,256]{0,1:T(8,128)(2,1)S(1)}, bf16[128,256]{0,1:T(8,128)(2,1)S(1)}, u32[]{:S(2)}, u32[]{:S(2)}) collective-permute-start(bf16[128,256]{0,1:T(8,128)(2,1)S(1)} %copy.23), channel_id=1, source_target_pairs={{0,1},{1,0},{2,3},{3,2},{4,5},{5,4},{6,7},{7,6},{8,9},{9,8},{10,11... | collective-permute-start | bytes 196616 | tf_op jit(solution)/shard_map/ppermute | solution.py:19
  49.4 7.4 %all-to-all-done.1 = bf16[4,32,4096]{2,1,0:T(8,128)(2,1)S(1)} async-done(((bf16[4,32,4096]{2,1,0:T(8,128)(2,1)}), bf16[4,32,4096]{2,1,0:T(8,128)(2,1)S(1)}, u32[]{:S(2)}, u32[]{:S(2)}) %all-to-all-start.1) | async-done | bytes 1048608 | tf_op jit(solution)/shard_map/all_to_all | solution.py:23
  56.8 0.2 convert_reduce_fusion
  57.0 1.2 select_add_fusion
  58.2 0.0 collective-permute-done.1
  58.2 0.2 copy.19
  58.4 0.2 reshape.60
  58.6 0.8 reverse_select_fusion.1
  59.4 6.4 %all-to-all-start.2 = ((bf16[8,32,512]{2,1,0:T(8,128)(2,1)}), bf16[8,32,512]{2,1,0:T(8,128)(2,1)S(1)}, u32[]{:S(2)}, u32[]{:S(2)}) async-start(bf16[8,32,512]{2,1,0:T(8,128)(2,1)} %reverse_select_fusion.1), calls=%async_computation.2 | async-start | bytes 524288 | tf_op jit(solution)/shard_map/all_to_all | solution.py:23
  65.8 15.7 %all-to-all-done.2 = bf16[8,32,512]{2,1,0:T(8,128)(2,1)S(1)} async-done(((bf16[8,32,512]{2,1,0:T(8,128)(2,1)}), bf16[8,32,512]{2,1,0:T(8,128)(2,1)S(1)}, u32[]{:S(2)}, u32[]{:S(2)}) %all-to-all-start.2) | async-done | bytes 262176 | tf_op jit(solution)/shard_map/all_to_all | solution.py:23
  81.5 2.7 %collective-permute-start.2 = (f32[32,256]{1,0:T(8,128)S(1)}, f32[32,256]{1,0:T(8,128)S(1)}, u32[]{:S(2)}, u32[]{:S(2)}) collective-permute-start(f32[32,256]{1,0:T(8,128)S(1)} %get-tuple-element.27), channel_id=1, source_target_pairs={{0,64},{64,0},{2,66},{66,2},{4,68},{68,4},{6,70},{70,6},{8,72},{72... | collective-permute-start | bytes 98312 | tf_op jit(solution)/shard_map/ppermute | solution.py:42
  84.2 4.5 %collective-permute-start.3 = (f32[32,256]{1,0:T(8,128)S(1)}, f32[32,256]{1,0:T(8,128)S(1)}, u32[]{:S(2)}, u32[]{:S(2)}) collective-permute-start(f32[32,256]{1,0:T(8,128)S(1)} %get-tuple-element.26), channel_id=1, source_target_pairs={{64,128},{128,64},{66,130},{130,66},{68,132},{132,68},{70,134},{13... | collective-permute-start | bytes 98312 | tf_op jit(solution)/shard_map/ppermute | solution.py:42
  88.8 0.0 collective-permute-done.2
  88.8 4.6 %collective-permute-done.3 = f32[32,256]{1,0:T(8,128)S(1)} collective-permute-done((f32[32,256]{1,0:T(8,128)S(1)}, f32[32,256]{1,0:T(8,128)S(1)}, u32[]{:S(2)}, u32[]{:S(2)}) %collective-permute-start.3) | collective-permute-done | bytes 32800 | tf_op jit(solution)/shard_map/ppermute | solution.py:42
  93.4 22.3 %all_to_all.30 = bf16[8,32,512]{2,1,0:T(8,128)(2,1)S(1)} all-to-all(bf16[8,32,512]{2,1,0:T(8,128)(2,1)S(1)} %broadcast_in_dim.64), channel_id=1, replica_groups=mesh['zh'=2,'x'=4,'y'=4,'z'=8,'c'=2] {'z'}, dimensions={0} | all-to-all | bytes 524288 | tf_op jit(solution)/shard_map/all_to_all | solution.py:23
  115.7 0.1 broadcast_in_dim.65
  115.8 13.3 %all_to_all.31.error_ref = bf16[4,8,32,512]{3,2,1,0:T(8,128)(2,1)S(1)} all-to-all(bf16[4,8,32,512]{3,2,1,0:T(8,128)(2,1)S(1)} %broadcast_in_dim.65), channel_id=1, replica_groups=mesh['zh'=2,'x'=4,'y'=4,'z'=8,'c'=2] {'y'}, dimensions={0} | all-to-all | bytes 2097152 | tf_op jit(solution)/shard_map/all_to_all | solution.py:23
  129.1 1.9 %collective-permute-start.4 = (bf16[4,8,32,512]{3,2,1,0:T(8,128)(2,1)S(1)}, bf16[4,8,32,512]{3,2,1,0:T(8,128)(2,1)}, u32[]{:S(2)}, u32[]{:S(2)}) collective-permute-start(bf16[4,8,32,512]{3,2,1,0:T(8,128)(2,1)S(1)} %all_to_all.31.error_ref), channel_id=1, source_target_pairs={{0,1},{1,0},{2,3},{3,2},{4,5},{5,4},{6,7},{7,6},{8,9},{9,8},{10,11... | collective-permute-start | bytes 3145736 | tf_op jit(solution)/shard_map/ppermute | solution.py:19
  131.1 3.8 %shard_map.77 = bf16[128,512]{1,0:T(8,128)(2,1)S(1)} custom-call(bf16[4,8,32,512]{3,2,1,0:T(8,128)(2,1)S(1)} %all_to_all.31.error_ref, bf16[256,4096]{1,0:T(8,128)(2,1)S(1)} %bitcast.36, bf16[256,4096]{1,0:T(8,128)(2,1)S(1)} %bitcast.37, bf16[256,4096]{1,0:T(8,128)(2,1)} %collective-permute-done.refs_2_.refs_3_, ...), custom_call_target="tpu_custom_call" | custom-call | flops 536870912 | bytes 5242880 | tf_op jit(solution)/shard_map/pallas_call | solution.py:83
  134.9 0.7 reshape.61
  135.6 0.0 collective-permute-done.4.other_ref
  135.6 8.0 %all-to-all-start.5 = ((bf16[32,4,512]{2,1,0:T(4,128)(2,1)}), bf16[32,4,512]{2,1,0:T(4,128)(2,1)S(1)}, u32[]{:S(2)}, u32[]{:S(2)}) async-start(bf16[32,4,512]{2,1,0:T(4,128)(2,1)} %reshape.61), calls=%async_computation.5 | async-start | bytes 262144 | tf_op jit(solution)/shard_map/all_to_all | solution.py:23
  143.6 0.1 copy.22
  143.8 3.4 %shard_map.78 = bf16[2,256,2048]{2,1,0:T(8,128)(2,1)S(1)} custom-call(bf16[256,256]{1,0:T(8,128)(2,1)S(1)} %maximum_bitcast_fusion.feature_ref, bf16[4,8,32,512]{3,2,1,0:T(8,128)(2,1)S(1)} %all_to_all.31.error_ref, bf16[4,8,32,512]{3,2,1,0:T(8,128)(2,1)} %collective-permute-done.4.other_ref), custom_call_target="tpu_custom_call" | custom-call | flops 536870912 | bytes 4194304 | tf_op jit(solution)/shard_map/pallas_call | solution.py:113
  147.1 3.5 %copy.21 = bf16[1,256,2,2048]{3,2,1,0:T(2,128)(2,1)} copy(bf16[1,256,2,2048]{3,1,2,0:T(8,128)(2,1)S(1)} %bitcast.38) | data formatting | bytes 4194304
  150.6 7.9 %all-to-all-done.5 = bf16[32,4,512]{2,1,0:T(4,128)(2,1)S(1)} async-done(((bf16[32,4,512]{2,1,0:T(4,128)(2,1)}), bf16[32,4,512]{2,1,0:T(4,128)(2,1)S(1)}, u32[]{:S(2)}, u32[]{:S(2)}) %all-to-all-start.5) | async-done | bytes 131104 | tf_op jit(solution)/shard_map/all_to_all | solution.py:23
  158.6 0.1 reshape.62
  158.7 0.8 fusion.1
  (16 shorter events, 0.3 us)
Async XLA Ops:
  0.6 4.6 %copy-start = (bf16[1,4,32,128]{3,2,1,0:T(8,128)(2,1)S(1)}, bf16[1,4,32,128]{3,2,1,0:T(8,128)(2,1)}, u32[]{:S(2)}) copy-start(bf16[1,4,32,128]{3,2,1,0:T(8,128)(2,1)} %param.6) | copy-start | bytes 98308
  0.6 4.5 %copy-start.1 = (f32[1,16384]{1,0:T(1,128)S(1)}, f32[1,16384]{1,0:T(1,128)}, u32[]{:S(2)}) copy-start(f32[1,16384]{1,0:T(1,128)} %param.8) | copy-start | bytes 196612
  0.7 4.5 %copy-start.4 = (s32[1,4,32]{2,1,0:T(4,128)S(1)}, s32[1,4,32]{2,1,0:T(4,128)}, u32[]{:S(2)}) copy-start(s32[1,4,32]{2,1,0:T(4,128)} %param.7) | copy-start | bytes 1540
  3.2 34.3 %collective-permute-start = (bf16[256,4096]{1,0:T(8,128)(2,1)S(1)}, bf16[256,4096]{1,0:T(8,128)(2,1)}, u32[]{:S(2)}, u32[]{:S(2)}) collective-permute-start(bf16[256,4096]{1,0:T(8,128)(2,1)S(1)} %bitcast.34), channel_id=1, source_target_pairs={{0,1},{1,0},{2,3},{3,2},{4,5},{5,4},{6,7},{7,6},{8,9},{9,8},{10,11... | collective-permute-start | bytes 6291464 | tf_op jit(solution)/shard_map/ppermute | solution.py:19
  6.5 30.5 %all-to-all-start = ((bf16[32,4,512]{2,1,0:T(4,128)(2,1)}), bf16[32,4,512]{2,1,0:T(4,128)(2,1)S(1)}, u32[]{:S(2)}, u32[]{:S(2)}) async-start(bf16[32,4,512]{2,1,0:T(4,128)(2,1)} %bitcast.33), calls=%async_computation | async-start | bytes 262144 | tf_op jit(solution)/shard_map/all_to_all | solution.py:23
  40.5 3.7 %copy-start.2 = (bf16[1,4,2048]{2,1,0:T(4,128)(2,1)S(1)}, bf16[1,4,2048]{2,1,0:T(4,128)(2,1)}, u32[]{:S(2)}) copy-start(bf16[1,4,2048]{2,1,0:T(4,128)(2,1)} %param.11) | copy-start | bytes 49156
  40.6 3.7 %copy-start.3 = (f32[1,2048]{1,0:T(1,128)S(1)}, f32[1,2048]{1,0:T(1,128)}, u32[]{:S(2)}) copy-start(f32[1,2048]{1,0:T(1,128)} %param.10) | copy-start | bytes 24580
  40.6 16.3 %all-to-all-start.1 = ((bf16[4,32,4096]{2,1,0:T(8,128)(2,1)}), bf16[4,32,4096]{2,1,0:T(8,128)(2,1)S(1)}, u32[]{:S(2)}, u32[]{:S(2)}) async-start(bf16[4,32,4096]{2,1,0:T(8,128)(2,1)} %bitcast.39), calls=%async_computation.1 | async-start | bytes 2097152 | tf_op jit(solution)/shard_map/all_to_all | solution.py:23
  47.5 10.7 %collective-permute-start.1 = (bf16[128,256]{0,1:T(8,128)(2,1)S(1)}, bf16[128,256]{0,1:T(8,128)(2,1)S(1)}, u32[]{:S(2)}, u32[]{:S(2)}) collective-permute-start(bf16[128,256]{0,1:T(8,128)(2,1)S(1)} %copy.23), channel_id=1, source_target_pairs={{0,1},{1,0},{2,3},{3,2},{4,5},{5,4},{6,7},{7,6},{8,9},{9,8},{10,11... | collective-permute-start | bytes 196616 | tf_op jit(solution)/shard_map/ppermute | solution.py:19
  59.4 22.1 %all-to-all-start.2 = ((bf16[8,32,512]{2,1,0:T(8,128)(2,1)}), bf16[8,32,512]{2,1,0:T(8,128)(2,1)S(1)}, u32[]{:S(2)}, u32[]{:S(2)}) async-start(bf16[8,32,512]{2,1,0:T(8,128)(2,1)} %reverse_select_fusion.1), calls=%async_computation.2 | async-start | bytes 524288 | tf_op jit(solution)/shard_map/all_to_all | solution.py:23
  81.5 7.3 %collective-permute-start.2 = (f32[32,256]{1,0:T(8,128)S(1)}, f32[32,256]{1,0:T(8,128)S(1)}, u32[]{:S(2)}, u32[]{:S(2)}) collective-permute-start(f32[32,256]{1,0:T(8,128)S(1)} %get-tuple-element.27), channel_id=1, source_target_pairs={{0,64},{64,0},{2,66},{66,2},{4,68},{68,4},{6,70},{70,6},{8,72},{72... | collective-permute-start | bytes 98312 | tf_op jit(solution)/shard_map/ppermute | solution.py:42
  84.2 9.1 %collective-permute-start.3 = (f32[32,256]{1,0:T(8,128)S(1)}, f32[32,256]{1,0:T(8,128)S(1)}, u32[]{:S(2)}, u32[]{:S(2)}) collective-permute-start(f32[32,256]{1,0:T(8,128)S(1)} %get-tuple-element.26), channel_id=1, source_target_pairs={{64,128},{128,64},{66,130},{130,66},{68,132},{132,68},{70,134},{13... | collective-permute-start | bytes 98312 | tf_op jit(solution)/shard_map/ppermute | solution.py:42
  129.1 6.5 %collective-permute-start.4 = (bf16[4,8,32,512]{3,2,1,0:T(8,128)(2,1)S(1)}, bf16[4,8,32,512]{3,2,1,0:T(8,128)(2,1)}, u32[]{:S(2)}, u32[]{:S(2)}) collective-permute-start(bf16[4,8,32,512]{3,2,1,0:T(8,128)(2,1)S(1)} %all_to_all.31.error_ref), channel_id=1, source_target_pairs={{0,1},{1,0},{2,3},{3,2},{4,5},{5,4},{6,7},{7,6},{8,9},{9,8},{10,11... | collective-permute-start | bytes 3145736 | tf_op jit(solution)/shard_map/ppermute | solution.py:19
  135.6 23.0 %all-to-all-start.5 = ((bf16[32,4,512]{2,1,0:T(4,128)(2,1)}), bf16[32,4,512]{2,1,0:T(4,128)(2,1)S(1)}, u32[]{:S(2)}, u32[]{:S(2)}) async-start(bf16[32,4,512]{2,1,0:T(4,128)(2,1)} %reshape.61), calls=%async_computation.5 | async-start | bytes 262144 | tf_op jit(solution)/shard_map/all_to_all | solution.py:23

commit v5 on v4

--- a/solution.py
+++ b/solution.py
@@ -23,6 +23,14 @@
     return lax.all_to_all(block, axis, split_axis=0, concat_axis=0, tiled=True)
 
 
+def exchange_z(block):
+    nz = SIZES[3]
+    order = [list(range(i * nz, (i + 1) * nz))[:: -1 if i % 2 else 1] for i in range(SIZES[0])]
+    return lax.all_to_all(
+        block, ("zh", "z"), split_axis=0, concat_axis=0, axis_index_groups=order, tiled=True
+    )
+
+
 def gather(block, axis):
     copies = jnp.broadcast_to(block[None], (lax.axis_size(axis),) + block.shape)
     return exchange(copies, axis)
@@ -32,7 +40,7 @@
     layers, nz = SIZES[0] * SIZES[1], SIZES[3]
     even = lax.axis_index(SECTION) % 2 == 0
     rounds = []
-    for first, sent in ((0, jnp.where(even, beyond, mine)), (1, jnp.where(even, mine, beyond))):
+    for first, sent in ((1, jnp.where(even, mine, beyond)), (0, jnp.where(even, beyond, mine))):
         route = []
         for i in range(first, layers - 1, 2):
             far = (i + 1) % SIZES[1] == 0
@@ -40,7 +48,7 @@
                 here, there = i * nz + z, (i + 1) * nz + (nz - 1 - z if far else z)
                 route += [(here, there), (there, here)]
         rounds.append(lax.ppermute(sent, SECTION + ("z",), route))
-    lower, upper = lax.optimization_barrier(tuple(rounds))
+    upper, lower = rounds
     return jnp.where(even, upper, lower), jnp.where(even, lower, upper)
 
 
@@ -149,6 +157,7 @@
 
     weights = lax.optimization_barrier(decoder[0].reshape(feat_dev, nc * width))
     weights_other = swap_cores(weights)
+    weights_other = jnp.where(jnp.isnan(thresholds[0, 0]), jnp.zeros_like(weights), weights_other)
 
     part = jnp.dot(f_mine, weights, preferred_element_type=f32)
     part = part + jnp.dot(f_other, weights_other, preferred_element_type=f32)
@@ -160,19 +169,16 @@
     part = part + jnp.where(here, shift[None], 0.0).reshape(part.shape)
     f_swapped = swap_cores(f_other)
     part, f_swapped = lax.optimization_barrier((part, f_swapped))
-    mirrored = lax.axis_index("zh") % 2 == 1
     part = part.reshape(nz * tok, nc, nz, col).transpose(2, 0, 1, 3).astype(WIRE_Z)
     part = part.reshape(nz, nz * tok, nc * col)
-    part = jnp.where(mirrored, part[::-1], part)
-    part = jnp.sum(exchange(part, "z").astype(f32), axis=0)
+    part = jnp.sum(exchange_z(part).astype(f32), axis=0)
 
     mine, beyond = part[:, :col], part[:, col:]
     got, got_next = with_neighbours(mine, beyond)
     error_next = jnp.where(layer == last_layer, 0.0, beyond + got_next)
     error = jnp.concatenate([mine + got, error_next], axis=1).astype(bf16)
 
-    error = gather(error, "z").reshape(nz, nz * tok, nc * col)
-    error = jnp.where(mirrored, error[::-1], error)
+    error = exchange_z(jnp.broadcast_to(error[None], (nz,) + error.shape))
     error = gather(error, "y")
     error_other = swap_cores(error)
 

time: 160 us -> 157 us (0.981)
  waiting for transfers between devices: 50.6 us -> 48 us
    all_to_all x2 -> x1, blocking collectives: 35.6 us -> 13.3 us  [exchange(): return lax.all_to_all(block, axis, split_axis=0, concat_axis=0, tiled=True)]
    all_to_all x0 -> x1, blocking collectives: none -> 21.7 us  [exchange_z(): lax.all_to_all(block, ('zh', 'z'), split_axis=0, concat_axis=0, axis_inde...]
    all_to_all x4 -> x3, waiting for transfers between devices: 46 us -> 28.5 us  [exchange(): return lax.all_to_all(block, axis, split_axis=0, concat_axis=0, tiled=True)]
    all_to_all x0 -> x1, waiting for transfers between devices: none -> 15.7 us  [exchange_z(): lax.all_to_all(block, ('zh', 'z'), split_axis=0, concat_axis=0, axis_inde...]
    all_to_all x0 -> x1, starting transfers between devices: none -> 6.4 us  [exchange_z(): lax.all_to_all(block, ('zh', 'z'), split_axis=0, concat_axis=0, axis_inde...]
    all_to_all x4 -> x3, starting transfers between devices: 33.6 us -> 27.5 us  [exchange(): return lax.all_to_all(block, axis, split_axis=0, concat_axis=0, tiled=True)]
    unnamed x16 -> x20, local copies, waits for them, and re-layouts: 6.3 us -> 6.31 us
  transfers between devices with their start and end apart: 9 -> 9, of which waited for: 5 -> 6; matrix products, arithmetic and copies ran while one was open for 7% -> 7% of each run, Pallas kernels for 5% -> 4%
where the time goes in v5:
time: 157 us; the launch traced here: 156 us
  waiting for transfers between devices  48 us (31%)
  starting transfers between devices  45.5 us (29%)
  blocking collectives  35 us (22%)
  local copies, waits for them, and re-layouts  12.8 us (8%)
  Pallas kernels  5.77 us (4%)
  other arithmetic  3.27 us (2%)
  matrix products  3.25 us (2%)
  between operations  2.3 us (1%)
    all_to_all x3, waiting for transfers between devices, exchange(): return lax.all_to_all(block, axis, split_axis=0, concat_axis=0, tiled=True)  28.5 us
    all_to_all x3, starting transfers between devices, exchange(): return lax.all_to_all(block, axis, split_axis=0, concat_axis=0, tiled=True)  27.5 us
    all_to_all x1, blocking collectives, exchange_z(): lax.all_to_all(block, ('zh', 'z'), split_axis=0, concat_axis=0, axis_inde...  21.7 us
    all_to_all x1, waiting for transfers between devices, exchange_z(): lax.all_to_all(block, ('zh', 'z'), split_axis=0, concat_axis=0, axis_inde...  15.7 us
    all_to_all x1, blocking collectives, exchange(): return lax.all_to_all(block, axis, split_axis=0, concat_axis=0, tiled=True)  13.3 us
    all_to_all x1, starting transfers between devices, exchange_z(): lax.all_to_all(block, ('zh', 'z'), split_axis=0, concat_axis=0, axis_inde...  6.4 us
    unnamed x20, local copies, waits for them, and re-layouts  6.31 us
    ppermute x2, starting transfers between devices, with_neighbours(): rounds.append(lax.ppermute(sent, SECTION + ('z',), route))  5.88 us
  transfers between devices with their start and end apart: 9, of which 6 were waited for; matrix products, arithmetic and copies ran while one was open for 7% of the time, Pallas kernels for 4%

profile of v5, /device:TPU:6, one launch (start us, length us, event | category | flops | bytes accessed | tf_op | source)
XLA Modules:
  0.0 156.0 jit_solution(3459548494132480921)
XLA Ops:
  0.6 0.0 copy-start
  0.6 0.0 copy-start.3
  0.7 0.0 copy-start.6
  0.7 2.5 %copy.24 = bf16[32,8,2,2048]{3,1,2,0:T(8,128)(2,1)S(1)} copy(bf16[32,8,2,2048]{3,2,1,0:T(2,128)(2,1)} %bitcast.41) | data formatting | bytes 4194304
  3.2 1.9 %collective-permute-start = (bf16[256,4096]{1,0:T(8,128)(2,1)S(1)}, bf16[256,4096]{1,0:T(8,128)(2,1)}, u32[]{:S(2)}, u32[]{:S(2)}) collective-permute-start(bf16[256,4096]{1,0:T(8,128)(2,1)S(1)} %bitcast.35), channel_id=1, source_target_pairs={{0,1},{1,0},{2,3},{3,2},{4,5},{5,4},{6,7},{7,6},{8,9},{9,8},{10,11... | collective-permute-start | bytes 6291464 | tf_op jit(solution)/shard_map/ppermute | solution.py:19
  5.1 0.0 copy-done.3
  5.2 0.0 copy-done
  5.2 0.0 copy-done.6
  5.2 0.3 fusion.10
  5.5 0.1 fusion.11
  5.6 0.1 reshape.58
  5.7 0.8 copy.27
  6.5 15.5 %all-to-all-start = ((bf16[32,4,512]{2,1,0:T(4,128)(2,1)}), bf16[32,4,512]{2,1,0:T(4,128)(2,1)S(1)}, u32[]{:S(2)}, u32[]{:S(2)}) async-start(bf16[32,4,512]{2,1,0:T(4,128)(2,1)} %bitcast.34), calls=%async_computation | async-start | bytes 262144 | tf_op jit(solution)/shard_map/all_to_all | solution.py:23
  22.0 0.5 slice.17
  23.8 13.1 %all-to-all-done = bf16[32,4,512]{2,1,0:T(4,128)(2,1)S(1)} async-done(((bf16[32,4,512]{2,1,0:T(4,128)(2,1)}), bf16[32,4,512]{2,1,0:T(4,128)(2,1)S(1)}, u32[]{:S(2)}, u32[]{:S(2)}) %all-to-all-start) | async-done | bytes 131104 | tf_op jit(solution)/shard_map/all_to_all | solution.py:23
  37.0 0.4 fusion.22
  37.5 0.0 collective-permute-done
  37.5 1.7 %broadcast_select_fusion.refs_2_.refs_3_ = bf16[256,4096]{1,0:T(8,128)(2,1)S(1)} fusion(bf16[256,4096]{1,0:T(8,128)(2,1)} %collective-permute-done, pred[]{:T(512)} %bitcast.5), kind=kLoop, calls=%fused_computation.3 | loop fusion | flops 1048576 | bytes 4194305 | tf_op jit(solution)/shard_map/jit(_where)/select_n | solution.py:160
  39.2 0.0 copy-start.1
  39.2 1.7 %fusion = bf16[128,4096]{1,0:T(8,128)(2,1)} fusion(f32[128,4096]{1,0:T(8,128)S(1)} %fusion.22, bf16[256,4096]{1,0:T(8,128)(2,1)S(1)} %broadcast_select_fusion.refs_2_.refs_3_, bf16[128,512]{1,0:T(8,128)(2,1)S(1)} %reshape.59), kind=kOutput, calls=%fused_computation.1 | convolution fusion | flops 269484032 | bytes 5308416 | tf_op jit(solution)/shard_map/dot_general | solution.py:163
  40.9 0.0 copy-done.1
  40.9 0.0 copy-start.4
  40.9 0.0 copy-start.5
  40.9 3.6 %all-to-all-start.1 = ((bf16[4,32,4096]{2,1,0:T(8,128)(2,1)}), bf16[4,32,4096]{2,1,0:T(8,128)(2,1)S(1)}, u32[]{:S(2)}, u32[]{:S(2)}) async-start(bf16[4,32,4096]{2,1,0:T(8,128)(2,1)} %bitcast.40), calls=%async_computation.1 | async-start | bytes 2097152 | tf_op jit(solution)/shard_map/all_to_all | solution.py:23
  44.5 0.0 copy-done.4
  44.5 0.0 copy-done.5
  44.6 0.9 broadcast_in_dim.64
  45.5 2.0 %broadcast_in_dim.65 = f32[32,4096]{1,0:T(8,128)} reshape(f32[8,4,4096]{2,1,0:T(4,128)} %broadcast_in_dim.64) | data formatting | bytes 1048576 | tf_op jit(solution)/shard_map/jit(_where)/broadcast_in_dim | solution.py:169
  47.5 0.1 broadcast_in_dim.61
  47.6 0.1 broadcast_in_dim.62
  47.7 0.1 copy.23
  47.8 1.9 %collective-permute-start.1 = (bf16[128,256]{0,1:T(8,128)(2,1)S(1)}, bf16[128,256]{0,1:T(8,128)(2,1)S(1)}, u32[]{:S(2)}, u32[]{:S(2)}) collective-permute-start(bf16[128,256]{0,1:T(8,128)(2,1)S(1)} %copy.23), channel_id=1, source_target_pairs={{0,1},{1,0},{2,3},{3,2},{4,5},{5,4},{6,7},{7,6},{8,9},{9,8},{10,11... | collective-permute-start | bytes 196616 | tf_op jit(solution)/shard_map/ppermute | solution.py:19
  49.8 7.4 %all-to-all-done.1 = bf16[4,32,4096]{2,1,0:T(8,128)(2,1)S(1)} async-done(((bf16[4,32,4096]{2,1,0:T(8,128)(2,1)}), bf16[4,32,4096]{2,1,0:T(8,128)(2,1)S(1)}, u32[]{:S(2)}, u32[]{:S(2)}) %all-to-all-start.1) | async-done | bytes 1048608 | tf_op jit(solution)/shard_map/all_to_all | solution.py:23
  57.2 0.2 convert_reduce_fusion
  57.3 1.2 select_add_fusion
  58.5 0.0 collective-permute-done.1
  58.5 0.2 copy.19
  58.8 0.9 reshape.61
  59.6 6.4 %all-to-all-start.2 = ((bf16[8,32,512]{2,1,0:T(8,128)(2,1)}), bf16[8,32,512]{2,1,0:T(8,128)(2,1)S(1)}, u32[]{:S(2)}, u32[]{:S(2)}) async-start(bf16[8,32,512]{2,1,0:T(8,128)(2,1)} %reshape.61), calls=%async_computation.2 | async-start | bytes 524288 | tf_op jit(solution)/shard_map/all_to_all | solution.py:29
  66.0 15.7 %all-to-all-done.2 = bf16[8,32,512]{2,1,0:T(8,128)(2,1)S(1)} async-done(((bf16[8,32,512]{2,1,0:T(8,128)(2,1)}), bf16[8,32,512]{2,1,0:T(8,128)(2,1)S(1)}, u32[]{:S(2)}, u32[]{:S(2)}) %all-to-all-start.2) | async-done | bytes 262176 | tf_op jit(solution)/shard_map/all_to_all | solution.py:29
  81.7 4.0 %collective-permute-start.2 = (f32[32,256]{1,0:T(8,128)S(1)}, f32[32,256]{1,0:T(8,128)S(1)}, u32[]{:S(2)}, u32[]{:S(2)}) collective-permute-start(f32[32,256]{1,0:T(8,128)S(1)} %get-tuple-element.22), channel_id=1, source_target_pairs={{64,128},{128,64},{66,130},{130,66},{68,132},{132,68},{70,134},{13... | collective-permute-start | bytes 98312 | tf_op jit(solution)/shard_map/ppermute | solution.py:50
  85.7 1.9 %collective-permute-start.3 = (f32[32,256]{1,0:T(8,128)S(1)}, f32[32,256]{1,0:T(8,128)S(1)}, u32[]{:S(2)}, u32[]{:S(2)}) collective-permute-start(f32[32,256]{1,0:T(8,128)S(1)} %get-tuple-element.23), channel_id=1, source_target_pairs={{0,64},{64,0},{2,66},{66,2},{4,68},{68,4},{6,70},{70,6},{8,72},{72... | collective-permute-start | bytes 98312 | tf_op jit(solution)/shard_map/ppermute | solution.py:50
  87.6 3.2 %collective-permute-done.2 = f32[32,256]{1,0:T(8,128)S(1)} collective-permute-done((f32[32,256]{1,0:T(8,128)S(1)}, f32[32,256]{1,0:T(8,128)S(1)}, u32[]{:S(2)}, u32[]{:S(2)}) %collective-permute-start.2) | collective-permute-done | bytes 32800 | tf_op jit(solution)/shard_map/ppermute | solution.py:50
  90.9 0.6 collective-permute-done.3
  91.5 0.0 copy-start.2
  91.6 21.7 %all_to_all.30 = bf16[8,32,512]{2,1,0:T(8,128)(2,1)S(1)} all-to-all(bf16[8,32,512]{2,1,0:T(8,128)(2,1)S(1)} %broadcast_in_dim.68), channel_id=1, replica_groups={{0,2,4,6,8,10,12,14},{270,268,266,264,262,260,258,256},{1,3,5,7,9,11,13..., dimensions={0} | all-to-all | bytes 524288 | tf_op jit(solution)/shard_map/all_to_all | solution.py:29
  113.3 0.1 broadcast_in_dim.69
  113.4 13.3 %all_to_all.31.error_ref = bf16[4,8,32,512]{3,2,1,0:T(8,128)(2,1)S(1)} all-to-all(bf16[4,8,32,512]{3,2,1,0:T(8,128)(2,1)S(1)} %broadcast_in_dim.69), channel_id=1, replica_groups=mesh['zh'=2,'x'=4,'y'=4,'z'=8,'c'=2] {'y'}, dimensions={0} | all-to-all | bytes 2097152 | tf_op jit(solution)/shard_map/all_to_all | solution.py:23
  126.8 1.9 %collective-permute-start.4 = (bf16[4,8,32,512]{3,2,1,0:T(8,128)(2,1)S(1)}, bf16[4,8,32,512]{3,2,1,0:T(8,128)(2,1)}, u32[]{:S(2)}, u32[]{:S(2)}) collective-permute-start(bf16[4,8,32,512]{3,2,1,0:T(8,128)(2,1)S(1)} %all_to_all.31.error_ref), channel_id=1, source_target_pairs={{0,1},{1,0},{2,3},{3,2},{4,5},{5,4},{6,7},{7,6},{8,9},{9,8},{10,11... | collective-permute-start | bytes 3145736 | tf_op jit(solution)/shard_map/ppermute | solution.py:19
  128.7 0.0 copy-done.2
  128.7 2.4 %shard_map.77 = bf16[128,512]{1,0:T(8,128)(2,1)S(1)} custom-call(bf16[4,8,32,512]{3,2,1,0:T(8,128)(2,1)S(1)} %all_to_all.31.error_ref, bf16[256,4096]{1,0:T(8,128)(2,1)S(1)} %bitcast.37, bf16[256,4096]{1,0:T(8,128)(2,1)S(1)} %bitcast.38, bf16[256,4096]{1,0:T(8,128)(2,1)S(1)} %copy-done.2, bf16[256,4096]{1,0:T(8,128)(2,1)S(1)} %copy-done.2), custom_call_target="tpu_custom_call" | custom-call | flops 536870912 | bytes 5242880 | tf_op jit(solution)/shard_map/pallas_call | solution.py:91
  131.1 0.7 reshape.62
  131.8 0.0 collective-permute-done.4.other_ref
  131.8 8.3 %all-to-all-start.5 = ((bf16[32,4,512]{2,1,0:T(4,128)(2,1)}), bf16[32,4,512]{2,1,0:T(4,128)(2,1)S(1)}, u32[]{:S(2)}, u32[]{:S(2)}) async-start(bf16[32,4,512]{2,1,0:T(4,128)(2,1)} %reshape.62), calls=%async_computation.5 | async-start | bytes 262144 | tf_op jit(solution)/shard_map/all_to_all | solution.py:23
  140.1 0.1 copy.22
  140.2 3.4 %shard_map.78 = bf16[2,256,2048]{2,1,0:T(8,128)(2,1)S(1)} custom-call(bf16[256,256]{1,0:T(8,128)(2,1)S(1)} %maximum_bitcast_fusion.feature_ref, bf16[4,8,32,512]{3,2,1,0:T(8,128)(2,1)S(1)} %all_to_all.31.error_ref, bf16[4,8,32,512]{3,2,1,0:T(8,128)(2,1)} %collective-permute-done.4.other_ref), custom_call_target="tpu_custom_call" | custom-call | flops 536870912 | bytes 4194304 | tf_op jit(solution)/shard_map/pallas_call | solution.py:121
  143.6 3.5 %copy.21 = bf16[1,256,2,2048]{3,2,1,0:T(2,128)(2,1)} copy(bf16[1,256,2,2048]{3,1,2,0:T(8,128)(2,1)S(1)} %bitcast.39) | data formatting | bytes 4194304
  147.1 7.9 %all-to-all-done.5 = bf16[32,4,512]{2,1,0:T(4,128)(2,1)S(1)} async-done(((bf16[32,4,512]{2,1,0:T(4,128)(2,1)}), bf16[32,4,512]{2,1,0:T(4,128)(2,1)S(1)}, u32[]{:S(2)}, u32[]{:S(2)}) %all-to-all-start.5) | async-done | bytes 131104 | tf_op jit(solution)/shard_map/all_to_all | solution.py:23
  155.1 0.1 reshape.63
  155.2 0.8 fusion.1
  (15 shorter events, 0.3 us)
Async XLA Ops:
  0.6 4.6 %copy-start = (bf16[1,4,32,128]{3,2,1,0:T(8,128)(2,1)S(1)}, bf16[1,4,32,128]{3,2,1,0:T(8,128)(2,1)}, u32[]{:S(2)}) copy-start(bf16[1,4,32,128]{3,2,1,0:T(8,128)(2,1)} %param.6) | copy-start | bytes 98308
  0.6 4.5 %copy-start.3 = (f32[1,16384]{1,0:T(1,128)S(1)}, f32[1,16384]{1,0:T(1,128)}, u32[]{:S(2)}) copy-start(f32[1,16384]{1,0:T(1,128)} %param.8) | copy-start | bytes 196612
  0.7 4.5 %copy-start.6 = (s32[1,4,32]{2,1,0:T(4,128)S(1)}, s32[1,4,32]{2,1,0:T(4,128)}, u32[]{:S(2)}) copy-start(s32[1,4,32]{2,1,0:T(4,128)} %param.7) | copy-start | bytes 1540
  3.2 34.3 %collective-permute-start = (bf16[256,4096]{1,0:T(8,128)(2,1)S(1)}, bf16[256,4096]{1,0:T(8,128)(2,1)}, u32[]{:S(2)}, u32[]{:S(2)}) collective-permute-start(bf16[256,4096]{1,0:T(8,128)(2,1)S(1)} %bitcast.35), channel_id=1, source_target_pairs={{0,1},{1,0},{2,3},{3,2},{4,5},{5,4},{6,7},{7,6},{8,9},{9,8},{10,11... | collective-permute-start | bytes 6291464 | tf_op jit(solution)/shard_map/ppermute | solution.py:19
  6.5 30.5 %all-to-all-start = ((bf16[32,4,512]{2,1,0:T(4,128)(2,1)}), bf16[32,4,512]{2,1,0:T(4,128)(2,1)S(1)}, u32[]{:S(2)}, u32[]{:S(2)}) async-start(bf16[32,4,512]{2,1,0:T(4,128)(2,1)} %bitcast.34), calls=%async_computation | async-start | bytes 262144 | tf_op jit(solution)/shard_map/all_to_all | solution.py:23
  39.2 1.7 %copy-start.1 = (bf16[256,4096]{1,0:T(8,128)(2,1)}, bf16[256,4096]{1,0:T(8,128)(2,1)S(1)}, u32[]{:S(2)}) copy-start(bf16[256,4096]{1,0:T(8,128)(2,1)S(1)} %broadcast_select_fusion.refs_2_.refs_3_) | copy-start | bytes 6291460
  40.9 3.7 %copy-start.4 = (bf16[1,4,2048]{2,1,0:T(4,128)(2,1)S(1)}, bf16[1,4,2048]{2,1,0:T(4,128)(2,1)}, u32[]{:S(2)}) copy-start(bf16[1,4,2048]{2,1,0:T(4,128)(2,1)} %param.11) | copy-start | bytes 49156
  40.9 3.7 %copy-start.5 = (f32[1,2048]{1,0:T(1,128)S(1)}, f32[1,2048]{1,0:T(1,128)}, u32[]{:S(2)}) copy-start(f32[1,2048]{1,0:T(1,128)} %param.10) | copy-start | bytes 24580
  40.9 16.3 %all-to-all-start.1 = ((bf16[4,32,4096]{2,1,0:T(8,128)(2,1)}), bf16[4,32,4096]{2,1,0:T(8,128)(2,1)S(1)}, u32[]{:S(2)}, u32[]{:S(2)}) async-start(bf16[4,32,4096]{2,1,0:T(8,128)(2,1)} %bitcast.40), calls=%async_computation.1 | async-start | bytes 2097152 | tf_op jit(solution)/shard_map/all_to_all | solution.py:23
  47.8 10.7 %collective-permute-start.1 = (bf16[128,256]{0,1:T(8,128)(2,1)S(1)}, bf16[128,256]{0,1:T(8,128)(2,1)S(1)}, u32[]{:S(2)}, u32[]{:S(2)}) collective-permute-start(bf16[128,256]{0,1:T(8,128)(2,1)S(1)} %copy.23), channel_id=1, source_target_pairs={{0,1},{1,0},{2,3},{3,2},{4,5},{5,4},{6,7},{7,6},{8,9},{9,8},{10,11... | collective-permute-start | bytes 196616 | tf_op jit(solution)/shard_map/ppermute | solution.py:19
  59.6 22.1 %all-to-all-start.2 = ((bf16[8,32,512]{2,1,0:T(8,128)(2,1)}), bf16[8,32,512]{2,1,0:T(8,128)(2,1)S(1)}, u32[]{:S(2)}, u32[]{:S(2)}) async-start(bf16[8,32,512]{2,1,0:T(8,128)(2,1)} %reshape.61), calls=%async_computation.2 | async-start | bytes 524288 | tf_op jit(solution)/shard_map/all_to_all | solution.py:29
  81.7 9.1 %collective-permute-start.2 = (f32[32,256]{1,0:T(8,128)S(1)}, f32[32,256]{1,0:T(8,128)S(1)}, u32[]{:S(2)}, u32[]{:S(2)}) collective-permute-start(f32[32,256]{1,0:T(8,128)S(1)} %get-tuple-element.22), channel_id=1, source_target_pairs={{64,128},{128,64},{66,130},{130,66},{68,132},{132,68},{70,134},{13... | collective-permute-start | bytes 98312 | tf_op jit(solution)/shard_map/ppermute | solution.py:50
  85.7 5.8 %collective-permute-start.3 = (f32[32,256]{1,0:T(8,128)S(1)}, f32[32,256]{1,0:T(8,128)S(1)}, u32[]{:S(2)}, u32[]{:S(2)}) collective-permute-start(f32[32,256]{1,0:T(8,128)S(1)} %get-tuple-element.23), channel_id=1, source_target_pairs={{0,64},{64,0},{2,66},{66,2},{4,68},{68,4},{6,70},{70,6},{8,72},{72... | collective-permute-start | bytes 98312 | tf_op jit(solution)/shard_map/ppermute | solution.py:50
  91.5 37.1 %copy-start.2 = (bf16[256,4096]{1,0:T(8,128)(2,1)S(1)}, bf16[256,4096]{1,0:T(8,128)(2,1)}, u32[]{:S(2)}) copy-start(bf16[256,4096]{1,0:T(8,128)(2,1)} %copy-done.1) | copy-start | bytes 6291460
  126.8 5.0 %collective-permute-start.4 = (bf16[4,8,32,512]{3,2,1,0:T(8,128)(2,1)S(1)}, bf16[4,8,32,512]{3,2,1,0:T(8,128)(2,1)}, u32[]{:S(2)}, u32[]{:S(2)}) collective-permute-start(bf16[4,8,32,512]{3,2,1,0:T(8,128)(2,1)S(1)} %all_to_all.31.error_ref), channel_id=1, source_target_pairs={{0,1},{1,0},{2,3},{3,2},{4,5},{5,4},{6,7},{7,6},{8,9},{9,8},{10,11... | collective-permute-start | bytes 3145736 | tf_op jit(solution)/shard_map/ppermute | solution.py:19
  131.8 23.2 %all-to-all-start.5 = ((bf16[32,4,512]{2,1,0:T(4,128)(2,1)}), bf16[32,4,512]{2,1,0:T(4,128)(2,1)S(1)}, u32[]{:S(2)}, u32[]{:S(2)}) async-start(bf16[32,4,512]{2,1,0:T(4,128)(2,1)} %reshape.62), calls=%async_computation.5 | async-start | bytes 262144 | tf_op jit(solution)/shard_map/all_to_all | solution.py:23

commit v6 on v5

--- a/solution.py
+++ b/solution.py
@@ -59,47 +59,104 @@
             yield z, r, block.reshape(-1, col)
 
 
-def grad_kernel(col, error_ref, *refs):
-    *weight_refs, grad_ref, total = refs
-    step = pl.program_id(0)
-    feat_dev = weight_refs[0].shape[0]
-
-    @pl.when(step == 0)
-    def _():
-        total[...] = jnp.zeros_like(total)
-
-    for z, r, block in column_blocks(error_ref, col):
-        for half in range(2):
-            weight = weight_refs[2 * half + r][:, z * col : (z + 1) * col]
-            total[:, half * feat_dev : (half + 1) * feat_dev] += lax.dot_general(
-                block, weight, (((1,), (1,)), ((), ())), preferred_element_type=jnp.float32
+def add_kernel(place_ref, part_ref, shift_ref, out_ref):
+    pieces, rows, both = out_ref.shape
+    col = both // 2
+    tok = shift_ref.shape[0]
+    own = lax.broadcasted_iota(jnp.int32, (rows, col), 0) - place_ref[0] * tok
+    for z in range(pieces):
+        for r in range(2):
+            start = (r * pieces + z) * col
+            total = part_ref[0, :, start : start + col].astype(jnp.float32)
+            for y in range(1, part_ref.shape[0]):
+                total += part_ref[y, :, start : start + col].astype(jnp.float32)
+            if r == 0:
+                for i in range(tok):
+                    shift = shift_ref[i : i + 1, start : start + col]
+                    total += jnp.where(own == i, shift, 0.0)
+            out_ref[z, :, r * col : (r + 1) * col] = total.astype(out_ref.dtype)
+
+
+def added(place, part, shift, pieces, dtype):
+    _, rows, columns = part.shape
+    return pl.pallas_call(
+        add_kernel,
+        in_specs=[
+            pl.BlockSpec(memory_space=pltpu.SMEM),
+            pl.BlockSpec(memory_space=pltpu.VMEM),
+            pl.BlockSpec(memory_space=pltpu.VMEM),
+        ],
+        out_specs=pl.BlockSpec(memory_space=pltpu.VMEM),
+        out_shape=jax.ShapeDtypeStruct((pieces, rows, columns // pieces), dtype),
+        compiler_params=pltpu.CompilerParams(vmem_limit_bytes=16 << 20),
+        cost_estimate=pl.CostEstimate(flops=part.size, bytes_accessed=2 << 20, transcendentals=0),
+    )(place, part, shift)
+
+
+def sum_kernel(feature_ref, mine_ref, other_ref, out_ref):
+    feat_dev, columns = mine_ref.shape
+    wide = 512
+    for start in range(0, columns, wide):
+        total = jnp.dot(
+            feature_ref[:, :feat_dev],
+            mine_ref[:, start : start + wide],
+            preferred_element_type=jnp.float32,
+        ) + jnp.dot(
+            feature_ref[:, feat_dev:],
+            other_ref[:, start : start + wide],
+            preferred_element_type=jnp.float32,
+        )
+        out_ref[:, start : start + wide] = total.astype(out_ref.dtype)
+
+
+def partial_sums(features, weights, weights_other, dtype):
+    tokens = features.shape[0]
+    return pl.pallas_call(
+        sum_kernel,
+        in_specs=[pl.BlockSpec(memory_space=pltpu.VMEM)] * 3,
+        out_specs=pl.BlockSpec(memory_space=pltpu.VMEM),
+        out_shape=jax.ShapeDtypeStruct((tokens, weights.shape[1]), dtype),
+        compiler_params=pltpu.CompilerParams(vmem_limit_bytes=24 << 20),
+        cost_estimate=pl.CostEstimate(
+            flops=4 * tokens * weights.size, bytes_accessed=1 << 20, transcendentals=0
+        ),
+    )(features, weights, weights_other)
+
+
+def grad_kernel(col, error_ref, mine_ref, other_ref, grad_ref, total):
+    feat_dev = mine_ref.shape[0]
+    pieces = error_ref.shape[1]
+    for half, weight_ref in enumerate((mine_ref, other_ref)):
+        place = slice(half * feat_dev, (half + 1) * feat_dev)
+        for z, r, block in column_blocks(error_ref, col):
+            start = (r * pieces + z) * col
+            term = lax.dot_general(
+                block,
+                weight_ref[:, start : start + col],
+                (((1,), (1,)), ((), ())),
+                preferred_element_type=jnp.float32,
             )
-
-    @pl.when(step == pl.num_programs(0) - 1)
-    def _():
-        grad_ref[...] = total[...].astype(grad_ref.dtype)
+            if z == 0 and r == 0:
+                total[:, place] = term
+            else:
+                total[:, place] += term
+    grad_ref[...] = total[...].astype(grad_ref.dtype)
 
 
 def feature_grads(error, weights, weights_other):
     ny, nz, rows, both = error.shape
     feat_dev = weights.shape[0]
-    steps = 4
-    wide = weights.shape[1] // 2 // steps
-    blocks = [
-        pl.BlockSpec((feat_dev, wide), lambda j, r=r: (0, r * steps + j)) for r in range(2)
-    ]
     return pl.pallas_call(
         functools.partial(grad_kernel, both // 2),
-        grid=(steps,),
-        in_specs=[pl.BlockSpec((ny, nz // steps, rows, both), lambda j: (0, j, 0, 0))] + 2 * blocks,
-        out_specs=pl.BlockSpec((ny * rows, 2 * feat_dev), lambda j: (0, 0)),
+        in_specs=[pl.BlockSpec(memory_space=pltpu.VMEM)] * 3,
+        out_specs=pl.BlockSpec(memory_space=pltpu.VMEM),
         out_shape=jax.ShapeDtypeStruct((ny * rows, 2 * feat_dev), error.dtype),
         scratch_shapes=[pltpu.VMEM((ny * rows, 2 * feat_dev), jnp.float32)],
         compiler_params=pltpu.CompilerParams(vmem_limit_bytes=24 << 20),
         cost_estimate=pl.CostEstimate(
-            flops=2 * error.size * 2 * feat_dev, bytes_accessed=5 << 20, transcendentals=0
+            flops=2 * error.size * 2 * feat_dev, bytes_accessed=1 << 20, transcendentals=0
         ),
-    )(error, weights, weights, weights_other, weights_other)
+    )(error, weights, weights_other)
 
 
 def decoder_kernel(col, feature_ref, error_ref, other_ref, out_ref):
@@ -157,20 +214,14 @@
 
     weights = lax.optimization_barrier(decoder[0].reshape(feat_dev, nc * width))
     weights_other = swap_cores(weights)
-    weights_other = jnp.where(jnp.isnan(thresholds[0, 0]), jnp.zeros_like(weights), weights_other)
-
-    part = jnp.dot(f_mine, weights, preferred_element_type=f32)
-    part = part + jnp.dot(f_other, weights_other, preferred_element_type=f32)
-    part = part.astype(WIRE_Y).reshape(ny, nz * tok, nc * width)
-    part = jnp.sum(exchange(part, "y").astype(f32), axis=0)
+
+    part = partial_sums(features, weights, weights_other, WIRE_Y)
+    part = part.reshape(ny, nz * tok, nc * width)
+    part = exchange(part, "y")
     shift = dec_bias[0][None, :] - targets[0].astype(f32)
-    shift = jnp.concatenate([shift, jnp.zeros_like(shift)], axis=1)
-    here = jnp.arange(nz)[:, None, None] == lax.axis_index("z")
-    part = part + jnp.where(here, shift[None], 0.0).reshape(part.shape)
+    part = added(lax.axis_index("z")[None], part, shift, nz, WIRE_Z)
     f_swapped = swap_cores(f_other)
     part, f_swapped = lax.optimization_barrier((part, f_swapped))
-    part = part.reshape(nz * tok, nc, nz, col).transpose(2, 0, 1, 3).astype(WIRE_Z)
-    part = part.reshape(nz, nz * tok, nc * col)
     part = jnp.sum(exchange_z(part).astype(f32), axis=0)
 
     mine, beyond = part[:, :col], part[:, col:]

time: 157 us -> 154 us (0.981)
  blocking collectives: 35 us -> 65.2 us
  starting transfers between devices: 45.5 us -> 30 us
  waiting for transfers between devices: 48 us -> 38 us
  local copies, waits for them, and re-layouts: 12.8 us -> 8.37 us
  Pallas kernels: 5.77 us -> 9.66 us
  other arithmetic: 3.27 us -> 0.21 us
  matrix products: 3.25 us -> 1.15 us
    all_to_all x1 -> x2, blocking collectives: 13.3 us -> 43.6 us  [exchange(): return lax.all_to_all(block, axis, split_axis=0, concat_axis=0, tiled=True)]
    all_to_all x3 -> x2, starting transfers between devices: 27.5 us -> 11.9 us  [exchange(): return lax.all_to_all(block, axis, split_axis=0, concat_axis=0, tiled=True)]
    all_to_all x3 -> x2, waiting for transfers between devices: 28.5 us -> 18.5 us  [exchange(): return lax.all_to_all(block, axis, split_axis=0, concat_axis=0, tiled=True)]
    pallas_call x1 -> x3, Pallas kernels: 2.41 us -> 6.3 us  [the longest x1 3.08 us: feature_grads(): pl.pallas_call(functools.partial(grad_kernel, both // 2), in_specs=[pl.Bl...]
    broadcast_in_dim x4 -> x0, local copies, waits for them, and re-layouts: 3.09 us -> none  [per_device(): part = part + jnp.where(here, shift[None], 0.0).reshape(part.shape)]
    dot_general x2 -> x0, matrix products: 2.1 us -> none  [the longest x1 1.65 us: per_device(): part = part + jnp.dot(f_other, weights_other, preferred_element_type=f32)]
    select_n x1 -> x0, other arithmetic: 1.74 us -> none  [per_device(): jnp.where(jnp.isnan(thresholds[0, 0]), jnp.zeros_like(weights), weights_o...]
    unnamed x20 -> x16, local copies, waits for them, and re-layouts: 6.31 us -> 7.2 us
  transfers between devices with their start and end apart: 9 -> 8, of which waited for: 6 -> 5; matrix products, arithmetic and copies ran while one was open for 7% -> 3% of each run, Pallas kernels for 4% -> 5%
where the time goes in v6:
time: 154 us
  blocking collectives  65.2 us (42%)
  waiting for transfers between devices  38 us (25%)
  starting transfers between devices  30 us (19%)
  Pallas kernels  9.66 us (6%)
  local copies, waits for them, and re-layouts  8.37 us (5%)
    all_to_all x2, blocking collectives, exchange(): return lax.all_to_all(block, axis, split_axis=0, concat_axis=0, tiled=True)  43.6 us
    all_to_all x1, blocking collectives, exchange_z(): lax.all_to_all(block, ('zh', 'z'), split_axis=0, concat_axis=0, axis_inde...  21.6 us
    all_to_all x2, waiting for transfers between devices, exchange(): return lax.all_to_all(block, axis, split_axis=0, concat_axis=0, tiled=True)  18.5 us
    all_to_all x1, waiting for transfers between devices, exchange_z(): lax.all_to_all(block, ('zh', 'z'), split_axis=0, concat_axis=0, axis_inde...  15.7 us
    all_to_all x2, starting transfers between devices, exchange(): return lax.all_to_all(block, axis, split_axis=0, concat_axis=0, tiled=True)  11.9 us
    unnamed x16, local copies, waits for them, and re-layouts  7.2 us
    all_to_all x1, starting transfers between devices, exchange_z(): lax.all_to_all(block, ('zh', 'z'), split_axis=0, concat_axis=0, axis_inde...  6.41 us
    ppermute x2, starting transfers between devices, with_neighbours(): rounds.append(lax.ppermute(sent, SECTION + ('z',), route))  5.88 us
  transfers between devices with their start and end apart: 8, of which 5 were waited for; matrix products, arithmetic and copies ran while one was open for 3% of the time, Pallas kernels for 5%

profile of v6, /device:TPU:6, one launch (start us, length us, event | category | flops | bytes accessed | tf_op | source)
XLA Modules:
  0.0 153.5 jit_solution(15158846077702794015)
XLA Ops:
  0.6 0.0 copy-start
  0.6 0.0 copy-start.2
  0.7 0.0 copy-start.5
  0.7 2.5 %copy.19 = bf16[32,8,2,2048]{3,1,2,0:T(8,128)(2,1)S(1)} copy(bf16[32,8,2,2048]{3,2,1,0:T(2,128)(2,1)} %bitcast.33) | data formatting | bytes 4194304
  3.2 1.9 %collective-permute-start = (bf16[256,4096]{1,0:T(8,128)(2,1)S(1)}, bf16[256,4096]{1,0:T(8,128)(2,1)}, u32[]{:S(2)}, u32[]{:S(2)}) collective-permute-start(bf16[256,4096]{1,0:T(8,128)(2,1)S(1)} %bitcast.28), channel_id=1, source_target_pairs={{0,1},{1,0},{2,3},{3,2},{4,5},{5,4},{6,7},{7,6},{8,9},{9,8},{10,11... | collective-permute-start | bytes 6291464 | tf_op jit(solution)/shard_map/ppermute | solution.py:19
  5.1 0.0 copy-done.2
  5.2 0.0 copy-done
  5.2 0.0 copy-done.5
  5.2 0.3 fusion.9
  5.5 0.1 fusion.10
  5.6 0.1 reshape.43
  5.7 0.1 copy.21
  5.8 30.3 %all_to_all.30 = bf16[32,4,512]{2,1,0:T(4,128)(2,1)S(1)} all-to-all(bf16[32,4,512]{2,1,0:T(4,128)(2,1)S(1)} %bitcast.35), channel_id=1, replica_groups=mesh['zh'=2,'x'=4,'y'=4,'z'=8,'c'=2] {'y','z'}, dimensions={0} | all-to-all | bytes 262144 | tf_op jit(solution)/shard_map/all_to_all | solution.py:23
  36.1 0.0 collective-permute-done.other_ref
  36.2 2.3 %shard_map.77 = bf16[128,4096]{1,0:T(8,128)(2,1)S(1)} custom-call(bf16[128,512]{1,0:T(8,128)(2,1)S(1)} %reshape.44.feature_ref, bf16[256,4096]{1,0:T(8,128)(2,1)S(1)} %bitcast.29, bf16[256,4096]{1,0:T(8,128)(2,1)} %collective-permute-done.other_ref), custom_call_target="tpu_custom_call" | custom-call | flops 536870912 | bytes 1048576 | tf_op jit(solution)/shard_map/pallas_call | solution.py:114
  38.5 0.0 copy-start.1
  38.5 1.0 copy-done.1
  39.5 0.0 copy-start.3
  39.5 0.0 copy-start.4
  39.5 3.6 %all-to-all-start.1 = ((bf16[4,32,4096]{2,1,0:T(8,128)(2,1)}), bf16[4,32,4096]{2,1,0:T(8,128)(2,1)S(1)}, u32[]{:S(2)}, u32[]{:S(2)}) async-start(bf16[4,32,4096]{2,1,0:T(8,128)(2,1)} %bitcast.32), calls=%async_computation.1 | async-start | bytes 2097152 | tf_op jit(solution)/shard_map/all_to_all | solution.py:23
  43.1 0.1 copy.17
  43.3 1.9 %collective-permute-start.1 = (bf16[128,256]{0,1:T(8,128)(2,1)S(1)}, bf16[128,256]{0,1:T(8,128)(2,1)S(1)}, u32[]{:S(2)}, u32[]{:S(2)}) collective-permute-start(bf16[128,256]{0,1:T(8,128)(2,1)S(1)} %copy.17), channel_id=1, source_target_pairs={{0,1},{1,0},{2,3},{3,2},{4,5},{5,4},{6,7},{7,6},{8,9},{9,8},{10,11... | collective-permute-start | bytes 196616 | tf_op jit(solution)/shard_map/ppermute | solution.py:19
  45.2 0.0 copy-done.3
  45.2 0.0 copy-done.4
  45.2 10.5 %all-to-all-done.1.part_ref = bf16[4,32,4096]{2,1,0:T(8,128)(2,1)S(1)} async-done(((bf16[4,32,4096]{2,1,0:T(8,128)(2,1)}), bf16[4,32,4096]{2,1,0:T(8,128)(2,1)S(1)}, u32[]{:S(2)}, u32[]{:S(2)}) %all-to-all-start.1) | async-done | bytes 1048608 | tf_op jit(solution)/shard_map/all_to_all | solution.py:23
  55.7 0.9 shard_map.78
  56.6 0.0 collective-permute-done.1
  56.6 6.4 %all-to-all-start.2 = ((bf16[8,32,512]{2,1,0:T(8,128)(2,1)}), bf16[8,32,512]{2,1,0:T(8,128)(2,1)S(1)}, u32[]{:S(2)}, u32[]{:S(2)}) async-start(bf16[8,32,512]{2,1,0:T(8,128)(2,1)} %shard_map.78), calls=%async_computation.2 | async-start | bytes 524288 | tf_op jit(solution)/shard_map/all_to_all | solution.py:29
  63.0 15.7 %all-to-all-done.2 = bf16[8,32,512]{2,1,0:T(8,128)(2,1)S(1)} async-done(((bf16[8,32,512]{2,1,0:T(8,128)(2,1)}), bf16[8,32,512]{2,1,0:T(8,128)(2,1)S(1)}, u32[]{:S(2)}, u32[]{:S(2)}) %all-to-all-start.2) | async-done | bytes 262176 | tf_op jit(solution)/shard_map/all_to_all | solution.py:29
  78.8 4.0 %collective-permute-start.2 = (f32[32,256]{1,0:T(8,128)S(1)}, f32[32,256]{1,0:T(8,128)S(1)}, u32[]{:S(2)}, u32[]{:S(2)}) collective-permute-start(f32[32,256]{1,0:T(8,128)S(1)} %get-tuple-element.20), channel_id=1, source_target_pairs={{64,128},{128,64},{66,130},{130,66},{68,132},{132,68},{70,134},{13... | collective-permute-start | bytes 98312 | tf_op jit(solution)/shard_map/ppermute | solution.py:50
  82.7 1.9 %collective-permute-start.3 = (f32[32,256]{1,0:T(8,128)S(1)}, f32[32,256]{1,0:T(8,128)S(1)}, u32[]{:S(2)}, u32[]{:S(2)}) collective-permute-start(f32[32,256]{1,0:T(8,128)S(1)} %get-tuple-element.21), channel_id=1, source_target_pairs={{0,64},{64,0},{2,66},{66,2},{4,68},{68,4},{6,70},{70,6},{8,72},{72... | collective-permute-start | bytes 98312 | tf_op jit(solution)/shard_map/ppermute | solution.py:50
  84.7 3.2 %collective-permute-done.2 = f32[32,256]{1,0:T(8,128)S(1)} collective-permute-done((f32[32,256]{1,0:T(8,128)S(1)}, f32[32,256]{1,0:T(8,128)S(1)}, u32[]{:S(2)}, u32[]{:S(2)}) %collective-permute-start.2) | collective-permute-done | bytes 32800 | tf_op jit(solution)/shard_map/ppermute | solution.py:50
  87.9 0.7 collective-permute-done.3
  88.6 21.6 %all_to_all.31 = bf16[8,32,512]{2,1,0:T(8,128)(2,1)S(1)} all-to-all(bf16[8,32,512]{2,1,0:T(8,128)(2,1)S(1)} %broadcast_in_dim.33), channel_id=1, replica_groups={{0,2,4,6,8,10,12,14},{270,268,266,264,262,260,258,256},{1,3,5,7,9,11,13..., dimensions={0} | all-to-all | bytes 524288 | tf_op jit(solution)/shard_map/all_to_all | solution.py:29
  110.2 0.1 broadcast_in_dim.34
  110.3 13.3 %all_to_all.32.error_ref = bf16[4,8,32,512]{3,2,1,0:T(8,128)(2,1)S(1)} all-to-all(bf16[4,8,32,512]{3,2,1,0:T(8,128)(2,1)S(1)} %broadcast_in_dim.34), channel_id=1, replica_groups=mesh['zh'=2,'x'=4,'y'=4,'z'=8,'c'=2] {'y'}, dimensions={0} | all-to-all | bytes 2097152 | tf_op jit(solution)/shard_map/all_to_all | solution.py:23
  123.6 1.9 %collective-permute-start.4 = (bf16[4,8,32,512]{3,2,1,0:T(8,128)(2,1)S(1)}, bf16[4,8,32,512]{3,2,1,0:T(8,128)(2,1)}, u32[]{:S(2)}, u32[]{:S(2)}) collective-permute-start(bf16[4,8,32,512]{3,2,1,0:T(8,128)(2,1)S(1)} %all_to_all.32.error_ref), channel_id=1, source_target_pairs={{0,1},{1,0},{2,3},{3,2},{4,5},{5,4},{6,7},{7,6},{8,9},{9,8},{10,11... | collective-permute-start | bytes 3145736 | tf_op jit(solution)/shard_map/ppermute | solution.py:19
  125.5 3.1 %shard_map.79 = bf16[128,512]{1,0:T(8,128)(2,1)S(1)} custom-call(bf16[4,8,32,512]{3,2,1,0:T(8,128)(2,1)S(1)} %all_to_all.32.error_ref, bf16[256,4096]{1,0:T(8,128)(2,1)S(1)} %bitcast.30, bf16[256,4096]{1,0:T(8,128)(2,1)} %collective-permute-done.other_ref), custom_call_target="tpu_custom_call" | custom-call | flops 536870912 | bytes 1048576 | tf_op jit(solution)/shard_map/pallas_call | solution.py:149
  128.6 0.7 reshape.46
  129.3 0.0 collective-permute-done.4.other_ref
  129.3 8.3 %all-to-all-start.5 = ((bf16[32,4,512]{2,1,0:T(4,128)(2,1)}), bf16[32,4,512]{2,1,0:T(4,128)(2,1)S(1)}, u32[]{:S(2)}, u32[]{:S(2)}) async-start(bf16[32,4,512]{2,1,0:T(4,128)(2,1)} %reshape.46), calls=%async_computation.5 | async-start | bytes 262144 | tf_op jit(solution)/shard_map/all_to_all | solution.py:23
  137.6 0.1 copy.18
  137.8 3.4 %shard_map.80 = bf16[2,256,2048]{2,1,0:T(8,128)(2,1)S(1)} custom-call(bf16[256,256]{1,0:T(8,128)(2,1)S(1)} %maximum_bitcast_fusion.feature_ref, bf16[4,8,32,512]{3,2,1,0:T(8,128)(2,1)S(1)} %all_to_all.32.error_ref, bf16[4,8,32,512]{3,2,1,0:T(8,128)(2,1)} %collective-permute-done.4.other_ref), custom_call_target="tpu_custom_call" | custom-call | flops 536870912 | bytes 4194304 | tf_op jit(solution)/shard_map/pallas_call | solution.py:178
  141.1 3.5 %copy.16 = bf16[1,256,2,2048]{3,2,1,0:T(2,128)(2,1)} copy(bf16[1,256,2,2048]{3,1,2,0:T(8,128)(2,1)S(1)} %bitcast.31) | data formatting | bytes 4194304
  144.6 7.9 %all-to-all-done.5 = bf16[32,4,512]{2,1,0:T(4,128)(2,1)S(1)} async-done(((bf16[32,4,512]{2,1,0:T(4,128)(2,1)}), bf16[32,4,512]{2,1,0:T(4,128)(2,1)S(1)}, u32[]{:S(2)}, u32[]{:S(2)}) %all-to-all-start.5) | async-done | bytes 131104 | tf_op jit(solution)/shard_map/all_to_all | solution.py:23
  152.6 0.1 reshape.47
  152.7 0.8 fusion
  (12 shorter events, 0.2 us)
Async XLA Ops:
  0.6 4.6 %copy-start = (bf16[1,4,32,128]{3,2,1,0:T(8,128)(2,1)S(1)}, bf16[1,4,32,128]{3,2,1,0:T(8,128)(2,1)}, u32[]{:S(2)}) copy-start(bf16[1,4,32,128]{3,2,1,0:T(8,128)(2,1)} %param.6) | copy-start | bytes 98308
  0.6 4.5 %copy-start.2 = (f32[1,16384]{1,0:T(1,128)S(1)}, f32[1,16384]{1,0:T(1,128)}, u32[]{:S(2)}) copy-start(f32[1,16384]{1,0:T(1,128)} %param.8) | copy-start | bytes 196612
  0.7 4.5 %copy-start.5 = (s32[1,4,32]{2,1,0:T(4,128)S(1)}, s32[1,4,32]{2,1,0:T(4,128)}, u32[]{:S(2)}) copy-start(s32[1,4,32]{2,1,0:T(4,128)} %param.7) | copy-start | bytes 1540
  3.2 33.0 %collective-permute-start = (bf16[256,4096]{1,0:T(8,128)(2,1)S(1)}, bf16[256,4096]{1,0:T(8,128)(2,1)}, u32[]{:S(2)}, u32[]{:S(2)}) collective-permute-start(bf16[256,4096]{1,0:T(8,128)(2,1)S(1)} %bitcast.28), channel_id=1, source_target_pairs={{0,1},{1,0},{2,3},{3,2},{4,5},{5,4},{6,7},{7,6},{8,9},{9,8},{10,11... | collective-permute-start | bytes 6291464 | tf_op jit(solution)/shard_map/ppermute | solution.py:19
  38.5 1.0 copy-start.1
  39.5 5.7 %copy-start.3 = (bf16[1,4,2048]{2,1,0:T(4,128)(2,1)S(1)}, bf16[1,4,2048]{2,1,0:T(4,128)(2,1)}, u32[]{:S(2)}) copy-start(bf16[1,4,2048]{2,1,0:T(4,128)(2,1)} %param.11) | copy-start | bytes 49156
  39.5 5.7 %copy-start.4 = (f32[1,2048]{1,0:T(1,128)S(1)}, f32[1,2048]{1,0:T(1,128)}, u32[]{:S(2)}) copy-start(f32[1,2048]{1,0:T(1,128)} %param.10) | copy-start | bytes 24580
  39.5 16.3 %all-to-all-start.1 = ((bf16[4,32,4096]{2,1,0:T(8,128)(2,1)}), bf16[4,32,4096]{2,1,0:T(8,128)(2,1)S(1)}, u32[]{:S(2)}, u32[]{:S(2)}) async-start(bf16[4,32,4096]{2,1,0:T(8,128)(2,1)} %bitcast.32), calls=%async_computation.1 | async-start | bytes 2097152 | tf_op jit(solution)/shard_map/all_to_all | solution.py:23
  43.3 13.4 %collective-permute-start.1 = (bf16[128,256]{0,1:T(8,128)(2,1)S(1)}, bf16[128,256]{0,1:T(8,128)(2,1)S(1)}, u32[]{:S(2)}, u32[]{:S(2)}) collective-permute-start(bf16[128,256]{0,1:T(8,128)(2,1)S(1)} %copy.17), channel_id=1, source_target_pairs={{0,1},{1,0},{2,3},{3,2},{4,5},{5,4},{6,7},{7,6},{8,9},{9,8},{10,11... | collective-permute-start | bytes 196616 | tf_op jit(solution)/shard_map/ppermute | solution.py:19
  56.6 22.1 %all-to-all-start.2 = ((bf16[8,32,512]{2,1,0:T(8,128)(2,1)}), bf16[8,32,512]{2,1,0:T(8,128)(2,1)S(1)}, u32[]{:S(2)}, u32[]{:S(2)}) async-start(bf16[8,32,512]{2,1,0:T(8,128)(2,1)} %shard_map.78), calls=%async_computation.2 | async-start | bytes 524288 | tf_op jit(solution)/shard_map/all_to_all | solution.py:29
  78.8 9.1 %collective-permute-start.2 = (f32[32,256]{1,0:T(8,128)S(1)}, f32[32,256]{1,0:T(8,128)S(1)}, u32[]{:S(2)}, u32[]{:S(2)}) collective-permute-start(f32[32,256]{1,0:T(8,128)S(1)} %get-tuple-element.20), channel_id=1, source_target_pairs={{64,128},{128,64},{66,130},{130,66},{68,132},{132,68},{70,134},{13... | collective-permute-start | bytes 98312 | tf_op jit(solution)/shard_map/ppermute | solution.py:50
  82.7 5.8 %collective-permute-start.3 = (f32[32,256]{1,0:T(8,128)S(1)}, f32[32,256]{1,0:T(8,128)S(1)}, u32[]{:S(2)}, u32[]{:S(2)}) collective-permute-start(f32[32,256]{1,0:T(8,128)S(1)} %get-tuple-element.21), channel_id=1, source_target_pairs={{0,64},{64,0},{2,66},{66,2},{4,68},{68,4},{6,70},{70,6},{8,72},{72... | collective-permute-start | bytes 98312 | tf_op jit(solution)/shard_map/ppermute | solution.py:50
  123.6 5.7 %collective-permute-start.4 = (bf16[4,8,32,512]{3,2,1,0:T(8,128)(2,1)S(1)}, bf16[4,8,32,512]{3,2,1,0:T(8,128)(2,1)}, u32[]{:S(2)}, u32[]{:S(2)}) collective-permute-start(bf16[4,8,32,512]{3,2,1,0:T(8,128)(2,1)S(1)} %all_to_all.32.error_ref), channel_id=1, source_target_pairs={{0,1},{1,0},{2,3},{3,2},{4,5},{5,4},{6,7},{7,6},{8,9},{9,8},{10,11... | collective-permute-start | bytes 3145736 | tf_op jit(solution)/shard_map/ppermute | solution.py:19
  129.3 23.2 %all-to-all-start.5 = ((bf16[32,4,512]{2,1,0:T(4,128)(2,1)}), bf16[32,4,512]{2,1,0:T(4,128)(2,1)S(1)}, u32[]{:S(2)}, u32[]{:S(2)}) async-start(bf16[32,4,512]{2,1,0:T(4,128)(2,1)} %reshape.46), calls=%async_computation.5 | async-start | bytes 262144 | tf_op jit(solution)/shard_map/all_to_all | solution.py:23
